TPU v7x, 256 devices: a whole 4x4x8 slice. The times are simulated.
256 devices in a mesh: theta: 128 (over z, x_lo, y, core), inst: 2 (over x_hi).
Axes of the slice: x: 4 (x_hi: 2, x_lo: 2; x = x_hi * 2 + x_lo), y: 4, z: 8, core: 2. Of those that a mesh axis runs over, the one named last changes fastest.
Arguments:
- coarse_state: float32 [5, 9, 65536], P(None, None, ('theta', 'inst')), may hold values from -6 to 6
- send_cells: int32 [256, 2048], P(('theta', 'inst')), may hold values from -1 to 255, as said below
- fine_source: int32 [2, 524288], P(None, ('theta', 'inst')), may hold values from 0 to 2047, as said below
- intersection_weight: float32 [524288], P(('theta', 'inst')), may hold values from 0.2 to 0.8
- neighbours: int32 [6, 524288], P(None, ('theta', 'inst')), may hold values from 0 to 3583, as said below
- face_area: float32 [6, 524288], P(None, ('theta', 'inst')), may hold values from 0.25 to 2
- time_step: float32 [524288], P(('theta', 'inst')), may hold values from 0.02 to 0.1
- face_mixing: float32 [6, 5, 5], replicated, may hold values from -0.75 to 1.2
- frequency: float32 [1], replicated, may hold values from 1 to 3
Outputs:
- fine_state: float32 [5, 9, 524288], P(None, None, ('theta', 'inst'))
Inputs may be any that keep to these rules, and one draw needn't show every extreme that they name: `send_cells`: entry [o, d * 8 + s] is the coarse cell of block o (numbered 0 to 255 within the block) that block o sends toward fine block d in slot s, or -1 where the slot is empty; the live slots of each pair come first, every pair has 1 to 8 live slots, and some fine block receives 8 live slots from every coarse block. `fine_source`: an entry o * 8 + s of a cell of fine block d names a live slot of send_cells[o] toward d; every live slot toward d is named by some cell of d. `neighbours`: A cell's own position in the extended list is 512 plus its index in the block. A position p below 3072 lies in layer p // 512 - 1, a position 3072 + q in layer q // 128; a cell of layer l names only positions of layers l - 1, l and l + 1, and positions at or above 3072 only of layer l.
All inputs are finite; a program needn't handle non-finite values.
Results may differ from a plain program's by a relative error of at most 0.0003.
Values sent between devices are 32-bit elements; how exact they have to be, the bound alone decides.
A program may use at most 128 MiB of HBM per device.

v0:
```python
import jax
import jax.numpy as jnp
from jax import lax
from jax.sharding import PartitionSpec as P

NV = 5
NI = 9
AXIAL = 128
RAD = 4
LAYERS = 4
RIM = 512
CELLS = 2048


SEGMENT_COEFS = (0.6, 0.6, 1.0)


def extended_2(cells, sides, width):
    for axis, dim in sides:
        count = lax.axis_size(axis)
        head = lax.slice_in_dim(cells, 0, width, axis=dim)
        tail = lax.slice_in_dim(cells, cells.shape[dim] - width, cells.shape[dim], axis=dim)
        cells = jnp.concatenate(
            [
                lax.ppermute(tail, axis, [(i, (i + 1) % count) for i in range(count)]),
                cells,
                lax.ppermute(head, axis, [((i + 1) % count, i) for i in range(count)]),
            ],
            axis=dim,
        )
    return cells


def from_partner(block, axis, distance):
    count = lax.axis_size(axis)
    route = []
    for low in range(count):
        high = low | 1 << distance
        if high != low and high < count:
            route += [(low, high), (high, low)]
    return lax.ppermute(block, axis, route)


def spectral_matrix(instances):
    index_row = jnp.arange(instances, dtype=jnp.int32)
    offsets = index_row[:, None] - index_row[None, :]
    parity = jnp.where(jnp.abs(offsets) % 2 == 0, 1.0, -1.0).astype(jnp.float32)
    angles = jnp.pi * offsets.astype(jnp.float32) / instances
    safe_sine = jnp.where(offsets == 0, 1.0, jnp.sin(angles))
    return jnp.where(offsets == 0, 0.0, 0.5 * parity / safe_sine)


def rate_rows(fields, extended, nbr_links, face_areas, mixing, omega_rate, time_deriv):
    cell_count = fields.shape[0]
    nearby = jnp.take(extended, nbr_links, axis=0)
    jumps = (nearby - fields[None, :, :]) * face_areas[:, :, None]
    jumps = jumps.reshape(6, cell_count, NV, NI)
    fluxes = jnp.einsum("kvw,kcwn->cvn", mixing, jumps, precision=lax.Precision.HIGHEST)
    spectral = jnp.einsum(
        "nm,cvm->cvn",
        time_deriv,
        fields.reshape(cell_count, NV, NI),
        precision=lax.Precision.HIGHEST,
    )
    return (omega_rate * spectral - fluxes).reshape(cell_count, NV * NI)


def cycle_layers(fields):
    return extended_2(fields, (("theta", 0),), RIM)


def radial_rows(fields):
    var_width = fields.shape[1]
    shaped = fields.reshape(LAYERS, RAD, AXIAL, var_width)
    facing = jnp.where(lax.axis_index("inst") == 0, shaped[:, RAD - 1], shaped[:, 0])
    return from_partner(facing.reshape(LAYERS * AXIAL, var_width), "inst", 0)


def per_device(
    coarse_state,
    send_cells,
    fine_source,
    intersection_weight,
    neighbours,
    face_area,
    time_step,
    face_mixing,
    frequency,
):
    var_width = NV * NI
    theta_count = lax.axis_size("theta")
    inst_count = lax.axis_size("inst")
    coarse_flat = coarse_state.reshape(var_width, coarse_state.shape[2])
    send_rows = jnp.maximum(send_cells[0], 0)
    capacity = send_rows.shape[0] // (theta_count * inst_count)
    outgoing = jnp.take(coarse_flat, send_rows, axis=1).reshape(
        var_width, theta_count, inst_count * capacity
    )
    incoming = lax.all_to_all(
        lax.all_to_all(outgoing, "theta", split_axis=1, concat_axis=1, tiled=True),
        "inst",
        split_axis=2,
        concat_axis=2,
        tiled=True,
    )
    received = incoming.reshape(var_width, theta_count * inst_count * capacity).T
    first_src = jnp.take(received, fine_source[0], axis=0)
    second_src = jnp.take(received, fine_source[1], axis=0)
    start_field = (
        intersection_weight[:, None] * first_src + (1.0 - intersection_weight[:, None]) * second_src
    )
    time_deriv = spectral_matrix(NI)
    omega_rate = frequency[0]
    current = start_field
    for segment_coef in SEGMENT_COEFS:
        across = radial_rows(current)
        cycle_ext = cycle_layers(current)
        full_ext = jnp.concatenate([cycle_ext, across], axis=0)
        rate_full = rate_rows(
            current, full_ext, neighbours, face_area, face_mixing, omega_rate, time_deriv
        )
        current = start_field - segment_coef * time_step[:, None] * rate_full
    return current.T.reshape(NV, NI, CELLS)


def solution(mesh):
    placed = (
        P(None, None, ("theta", "inst")),
        P(("theta", "inst"), None),
        P(None, ("theta", "inst")),
        P(("theta", "inst")),
        P(None, ("theta", "inst")),
        P(None, ("theta", "inst")),
        P(("theta", "inst")),
        P(),
        P(),
    )
    return jax.shard_map(
        per_device,
        mesh=mesh,
        in_specs=placed,
        out_specs=P(None, None, ("theta", "inst")),
        check_vma=False,
    )
```

profile of v0, /device:TPU:2, one launch (start us, length us, event | category | flops | bytes accessed | tf_op | source)
XLA Modules:
  0.0 274.8 jit_solution(5461588177477221418)
XLA Ops:
  2.6 5.5 %gather_fusion = f32[2048,45]{1,0:T(8,128)S(1)} fusion(f32[45,256]{0,1:T(8,128)S(1)} %copy.141, s32[2048]{0:T(1024)S(1)} %broadcast_clamp_fusion.1), kind=kCustom, calls=%fused_computation.5 | custom fusion | bytes 745472 | tf_op jit(solution)/shard_map/jit(_take)/gather | solution.py:96
  8.4 2.1 reshape.205
  10.5 14.0 %all-to-all-start = ((f32[128,1,720]{2,1,0:T(1,128)}), f32[128,1,720]{2,1,0:T(1,128)S(1)}, u32[]{:S(2)}, u32[]{:S(2)}) async-start(f32[128,1,720]{2,1,0:T(1,128)} %reshape.205), calls=%async_computation | async-start | bytes 786432 | tf_op jit(solution)/shard_map/all_to_all | solution.py:100
  24.7 15.9 %all-to-all-done = f32[128,1,720]{2,1,0:T(1,128)S(1)} async-done(((f32[128,1,720]{2,1,0:T(1,128)}), f32[128,1,720]{2,1,0:T(1,128)S(1)}, u32[]{:S(2)}, u32[]{:S(2)}) %all-to-all-start) | async-done | bytes 368672 | tf_op jit(solution)/shard_map/all_to_all | solution.py:100
  41.1 1.6 reduce.2
  44.7 3.5 %all-to-all-start.1 = ((f32[45,128,16]{1,0,2:T(8,128)}), f32[45,128,16]{1,0,2:T(8,128)S(1)}, u32[]{:S(2)}, u32[]{:S(2)}) async-start(f32[45,128,16]{1,0,2:T(8,128)} %copy.142), calls=%async_computation.1 | async-start | bytes 786432 | tf_op jit(solution)/shard_map/all_to_all | solution.py:99
  48.2 8.6 %all-to-all-done.1 = f32[45,128,16]{1,0,2:T(8,128)S(1)} async-done(((f32[45,128,16]{1,0,2:T(8,128)}), f32[45,128,16]{1,0,2:T(8,128)S(1)}, u32[]{:S(2)}, u32[]{:S(2)}) %all-to-all-start.1) | async-done | bytes 368672 | tf_op jit(solution)/shard_map/all_to_all | solution.py:99
  57.3 5.5 %gather_fusion.2 = f32[2048,45]{1,0:T(8,128)S(1)} fusion(f32[2048,45]{1,0:T(8,128)S(1)} %bitcast.97, s32[2048]{0:T(1024)S(1)} %fusion.17), kind=kCustom, calls=%fused_computation.2.clone | custom fusion | bytes 745472 | tf_op jit(solution)/shard_map/jit(_take)/gather | solution.py:108
  62.8 5.5 %gather_fusion.1 = f32[2048,45]{1,0:T(8,128)S(1)} fusion(f32[2048,45]{1,0:T(8,128)S(1)} %bitcast.98, s32[2048]{0:T(1024)S(1)} %fusion.16), kind=kCustom, calls=%fused_computation.clone | custom fusion | bytes 745472 | tf_op jit(solution)/shard_map/jit(_take)/gather | solution.py:107
  68.3 1.8 fusion.6
  70.6 3.9 %collective-permute-start.1 = (f32[512,45]{1,0:T(8,128)S(1)}, f32[512,45]{1,0:T(8,128)}, u32[]{:S(2)}, u32[]{:S(2)}) collective-permute-start(f32[512,45]{1,0:T(8,128)S(1)} %get-tuple-element.12), channel_id=1, source_target_pairs={{2,0},{4,2},{6,4},{8,6},{10,8},{12,10},{14,12},{16,14},{18,16},{20... | collective-permute-start | bytes 276488 | tf_op jit(solution)/shard_map/ppermute | solution.py:27
  76.5 2.8 %collective-permute-done.2 = f32[512,45]{1,0:T(8,128)S(1)} collective-permute-done((f32[512,45]{1,0:T(8,128)S(1)}, f32[512,45]{1,0:T(8,128)S(1)}, u32[]{:S(2)}, u32[]{:S(2)}) %collective-permute-start.2) | collective-permute-done | bytes 92192 | tf_op jit(solution)/shard_map/ppermute | solution.py:41
  82.1 41.1 %gather_fusion.3 = f32[12288,45]{1,0:T(8,128)} fusion(f32[3584,45]{1,0:T(8,128)S(1)} %pad_maximum_fusion, s32[12288]{0:T(1024)S(1)} %broadcast_clamp_fusion), kind=kCustom, calls=%fused_computation.1.clone | custom fusion | bytes 4472832 | tf_op jit(solution)/shard_map/jit(_take)/gather | solution.py:55
  123.2 6.4 %copy.147 = f32[6,2048,45]{1,0,2:T(8,128)} copy(f32[6,2048,45]{2,1,0:T(8,128)} %bitcast.101) | data formatting | bytes 4423680 | tf_op jit(solution)/shard_map/jit(_take)/gather | solution.py:55
  129.6 2.3 fusion.2
  132.0 2.0 convolution_bitcast_fusion.2
  137.2 2.3 collective-permute-start.5
  139.6 3.9 %collective-permute-start.4 = (f32[512,45]{1,0:T(8,128)S(1)}, f32[512,45]{1,0:T(8,128)}, u32[]{:S(2)}, u32[]{:S(2)}) collective-permute-start(f32[512,45]{1,0:T(8,128)S(1)} %get-tuple-element.10), channel_id=1, source_target_pairs={{2,0},{4,2},{6,4},{8,6},{10,8},{12,10},{14,12},{16,14},{18,16},{20... | collective-permute-start | bytes 276488 | tf_op jit(solution)/shard_map/ppermute | solution.py:27
  145.5 4.9 %collective-permute-done.3 = f32[512,45]{1,0:T(8,128)S(1)} collective-permute-done((f32[512,45]{1,0:T(8,128)}, f32[512,45]{1,0:T(8,128)S(1)}, u32[]{:S(2)}, u32[]{:S(2)}) %collective-permute-start.3) | collective-permute-done | bytes 92192 | tf_op jit(solution)/shard_map/ppermute | solution.py:25
  151.1 1.5 pad_maximum_fusion.1
  152.7 41.1 %gather_fusion.4 = f32[12288,45]{1,0:T(8,128)} fusion(f32[3584,45]{1,0:T(8,128)S(1)} %pad_maximum_fusion.1, s32[12288]{0:T(1024)S(1)} %broadcast_clamp_fusion), kind=kCustom, calls=%fused_computation.3.clone | custom fusion | bytes 4472832 | tf_op jit(solution)/shard_map/jit(_take)/gather | solution.py:55
  193.8 6.4 %copy.155 = f32[6,2048,45]{1,0,2:T(8,128)} copy(f32[6,2048,45]{2,1,0:T(8,128)} %bitcast.102) | data formatting | bytes 4423680 | tf_op jit(solution)/shard_map/jit(_take)/gather | solution.py:55
  200.1 2.3 fusion.1
  202.5 2.0 convolution_bitcast_fusion.1
  209.1 3.9 %collective-permute-start.7 = (f32[512,45]{1,0:T(8,128)S(1)}, f32[512,45]{1,0:T(8,128)}, u32[]{:S(2)}, u32[]{:S(2)}) collective-permute-start(f32[512,45]{1,0:T(8,128)S(1)} %get-tuple-element.8), channel_id=1, source_target_pairs={{2,0},{4,2},{6,4},{8,6},{10,8},{12,10},{14,12},{16,14},{18,16},{20... | collective-permute-start | bytes 276488 | tf_op jit(solution)/shard_map/ppermute | solution.py:27
  214.2 1.6 collective-permute-done.8
  215.8 1.7 collective-permute-done.6
  218.3 1.5 pad_maximum_fusion.2
  219.8 41.1 %gather_fusion.5 = f32[12288,45]{1,0:T(8,128)} fusion(f32[3584,45]{1,0:T(8,128)S(1)} %pad_maximum_fusion.2, s32[12288]{0:T(1024)S(1)} %broadcast_clamp_fusion), kind=kCustom, calls=%fused_computation.4.clone | custom fusion | bytes 4472832 | tf_op jit(solution)/shard_map/jit(_take)/gather | solution.py:55
  260.9 6.4 %copy.163 = f32[6,2048,45]{1,0,2:T(8,128)} copy(f32[6,2048,45]{2,1,0:T(8,128)} %bitcast.100) | data formatting | bytes 4423680 | tf_op jit(solution)/shard_map/jit(_take)/gather | solution.py:55
  267.3 2.3 fusion
  269.6 2.0 convolution_bitcast_fusion
  (95 shorter events, 26.3 us)
Async XLA Ops:
  8.1 16.5 %copy-start.12 = (s32[6,2048]{1,0:T(8,128)S(1)}, s32[6,2048]{1,0:T(8,128)}, u32[]{:S(2)}) copy-start(s32[6,2048]{1,0:T(8,128)} %param.17) | copy-start | bytes 147460
  8.1 16.5 %copy-start.16 = (s32[2,2048]{1,0:T(2,128)S(1)}, s32[2,2048]{1,0:T(2,128)}, u32[]{:S(2)}) copy-start(s32[2,2048]{1,0:T(2,128)} %param.15) | copy-start | bytes 49156
  10.5 37.7 %copy-start.13 = (f32[2048]{0:T(1024)S(1)}, f32[2048]{0:T(1024)}, u32[]{:S(2)}) copy-start(f32[2048]{0:T(1024)} %param.16) | copy-start | bytes 24580
  10.5 30.1 %all-to-all-start = ((f32[128,1,720]{2,1,0:T(1,128)}), f32[128,1,720]{2,1,0:T(1,128)S(1)}, u32[]{:S(2)}, u32[]{:S(2)}) async-start(f32[128,1,720]{2,1,0:T(1,128)} %reshape.205), calls=%async_computation | async-start | bytes 786432 | tf_op jit(solution)/shard_map/all_to_all | solution.py:100
  44.7 12.1 %all-to-all-start.1 = ((f32[45,128,16]{1,0,2:T(8,128)}), f32[45,128,16]{1,0,2:T(8,128)S(1)}, u32[]{:S(2)}, u32[]{:S(2)}) async-start(f32[45,128,16]{1,0,2:T(8,128)} %copy.142), calls=%async_computation.1 | async-start | bytes 786432 | tf_op jit(solution)/shard_map/all_to_all | solution.py:99
  68.3 6.2 %copy-start.14 = (f32[2048]{0:T(1024)S(1)}, f32[2048]{0:T(1024)}, u32[]{:S(2)}) copy-start(f32[2048]{0:T(1024)} %param.19) | copy-start | bytes 24580
  68.3 6.8 %copy-start.15 = (f32[6,5,5]{2,0,1:T(8,128)S(1)}, f32[6,5,5]{2,0,1:T(8,128)}, u32[]{:S(2)}) copy-start(f32[6,5,5]{2,0,1:T(8,128)} %param.20) | copy-start | bytes 1804
  70.2 9.1 %collective-permute-start.2 = (f32[512,45]{1,0:T(8,128)S(1)}, f32[512,45]{1,0:T(8,128)S(1)}, u32[]{:S(2)}, u32[]{:S(2)}) collective-permute-start(f32[512,45]{1,0:T(8,128)S(1)} %bitcast.110), channel_id=1, source_target_pairs={{0,1},{1,0},{2,3},{3,2},{4,5},{5,4},{6,7},{7,6},{8,9},{9,8},{10,11... | collective-permute-start | bytes 276488 | tf_op jit(solution)/shard_map/ppermute | solution.py:41
  70.6 9.6 %collective-permute-start = (f32[512,45]{1,0:T(8,128)S(1)}, f32[512,45]{1,0:T(8,128)S(1)}, u32[]{:S(2)}, u32[]{:S(2)}) collective-permute-start(f32[512,45]{1,0:T(8,128)S(1)} %get-tuple-element.11), channel_id=1, source_target_pairs={{0,2},{2,4},{4,6},{6,8},{8,10},{10,12},{12,14},{14,16},{16,18},{18... | collective-permute-start | bytes 276488 | tf_op jit(solution)/shard_map/ppermute | solution.py:25
  70.6 10.3 %collective-permute-start.1 = (f32[512,45]{1,0:T(8,128)S(1)}, f32[512,45]{1,0:T(8,128)}, u32[]{:S(2)}, u32[]{:S(2)}) collective-permute-start(f32[512,45]{1,0:T(8,128)S(1)} %get-tuple-element.12), channel_id=1, source_target_pairs={{2,0},{4,2},{6,4},{8,6},{10,8},{12,10},{14,12},{16,14},{18,16},{20... | collective-permute-start | bytes 276488 | tf_op jit(solution)/shard_map/ppermute | solution.py:27
  79.4 0.8 copy-start.6
  80.2 0.7 copy-start.9
  123.2 6.4 %copy-start.5 = (f32[6,2048]{1,0:T(8,128)S(1)}, f32[6,2048]{1,0:T(8,128)}, u32[]{:S(2)}) copy-start(f32[6,2048]{1,0:T(8,128)} %param.18) | copy-start | bytes 147460
  131.9 2.0 copy-start.4
  135.7 14.7 %copy-start.1 = (f32[2048,45]{1,0:T(8,128)}, f32[2048,45]{1,0:T(8,128)S(1)}, u32[]{:S(2)}) copy-start(f32[2048,45]{1,0:T(8,128)S(1)} %multiply_subtract_fusion.1) | copy-start | bytes 1105924
  137.2 8.2 %collective-permute-start.5 = (f32[512,45]{1,0:T(8,128)}, f32[512,45]{1,0:T(8,128)S(1)}, u32[]{:S(2)}, u32[]{:S(2)}) collective-permute-start(f32[512,45]{1,0:T(8,128)} %bitcast.18), channel_id=1, source_target_pairs={{0,1},{1,0},{2,3},{3,2},{4,5},{5,4},{6,7},{7,6},{8,9},{9,8},{10,11... | collective-permute-start | bytes 276488 | tf_op jit(solution)/shard_map/ppermute | solution.py:41
  139.5 10.9 %collective-permute-start.3 = (f32[512,45]{1,0:T(8,128)}, f32[512,45]{1,0:T(8,128)S(1)}, u32[]{:S(2)}, u32[]{:S(2)}) collective-permute-start(f32[512,45]{1,0:T(8,128)} %get-tuple-element.9), channel_id=1, source_target_pairs={{0,2},{2,4},{4,6},{6,8},{8,10},{10,12},{12,14},{14,16},{16,18},{18... | collective-permute-start | bytes 276488 | tf_op jit(solution)/shard_map/ppermute | solution.py:25
  139.6 11.6 %collective-permute-start.4 = (f32[512,45]{1,0:T(8,128)S(1)}, f32[512,45]{1,0:T(8,128)}, u32[]{:S(2)}, u32[]{:S(2)}) collective-permute-start(f32[512,45]{1,0:T(8,128)S(1)} %get-tuple-element.10), channel_id=1, source_target_pairs={{2,0},{4,2},{6,4},{8,6},{10,8},{12,10},{14,12},{16,14},{18,16},{20... | collective-permute-start | bytes 276488 | tf_op jit(solution)/shard_map/ppermute | solution.py:27
  145.5 5.0 %copy-start.7 = (f32[512,45]{1,0:T(8,128)}, f32[512,45]{1,0:T(8,128)S(1)}, u32[]{:S(2)}) copy-start(f32[512,45]{1,0:T(8,128)S(1)} %collective-permute-done.5) | copy-start | bytes 276484
  150.4 0.7 copy-start.10
  202.5 2.0 copy-start.3
  206.2 11.4 %copy-start = (f32[2048,45]{1,0:T(8,128)}, f32[2048,45]{1,0:T(8,128)S(1)}, u32[]{:S(2)}) copy-start(f32[2048,45]{1,0:T(8,128)S(1)} %multiply_subtract_fusion) | copy-start | bytes 1105924
  207.7 8.1 %collective-permute-start.8 = (f32[512,45]{1,0:T(8,128)}, f32[512,45]{1,0:T(8,128)S(1)}, u32[]{:S(2)}, u32[]{:S(2)}) collective-permute-start(f32[512,45]{1,0:T(8,128)} %bitcast.25), channel_id=1, source_target_pairs={{0,1},{1,0},{2,3},{3,2},{4,5},{5,4},{6,7},{7,6},{8,9},{9,8},{10,11... | collective-permute-start | bytes 276488 | tf_op jit(solution)/shard_map/ppermute | solution.py:41
  209.1 8.4 %collective-permute-start.6 = (f32[512,45]{1,0:T(8,128)}, f32[512,45]{1,0:T(8,128)S(1)}, u32[]{:S(2)}, u32[]{:S(2)}) collective-permute-start(f32[512,45]{1,0:T(8,128)} %get-tuple-element.6), channel_id=1, source_target_pairs={{0,2},{2,4},{4,6},{6,8},{8,10},{10,12},{12,14},{14,16},{16,18},{18... | collective-permute-start | bytes 276488 | tf_op jit(solution)/shard_map/ppermute | solution.py:25
  209.1 9.1 %collective-permute-start.7 = (f32[512,45]{1,0:T(8,128)S(1)}, f32[512,45]{1,0:T(8,128)}, u32[]{:S(2)}, u32[]{:S(2)}) collective-permute-start(f32[512,45]{1,0:T(8,128)S(1)} %get-tuple-element.8), channel_id=1, source_target_pairs={{2,0},{4,2},{6,4},{8,6},{10,8},{12,10},{14,12},{16,14},{18,16},{20... | collective-permute-start | bytes 276488 | tf_op jit(solution)/shard_map/ppermute | solution.py:27
  215.8 1.7 copy-start.8
  217.6 0.7 copy-start.11
  269.6 2.0 copy-start.2
where the time goes:
time: 279 us; the launch traced here: 275 us
  local copies, waits for them, and re-layouts  175 us (63%)
  waiting for transfers between devices  37.3 us (13%)
  starting transfers between devices  33.2 us (12%)
  other arithmetic  19.1 us (7%)
  matrix products  8.86 us (3%)
    gather x6, local copies, waits for them, and re-layouts, rate_rows(): nearby = jnp.take(extended, nbr_links, axis=0)  142 us
    all_to_all x1, waiting for transfers between devices, per_device(): lax.all_to_all(outgoing, 'theta', split_axis=1, concat_axis=1, tiled=True)  15.9 us
    all_to_all x1, starting transfers between devices, per_device(): lax.all_to_all(outgoing, 'theta', split_axis=1, concat_axis=1, tiled=True)  14 us
    ppermute x3, starting transfers between devices, extended_2(): lax.ppermute(head, axis, [((i + 1) % count, i) for i in range(count)])  11.6 us
    all_to_all x1, waiting for transfers between devices, per_device(): lax.all_to_all(lax.all_to_all(outgoing, 'theta', split_axis=1, concat_axi...  8.65 us
    ppermute x3, waiting for transfers between devices, extended_2(): lax.ppermute(tail, axis, [(i, (i + 1) % count) for i in range(count)])  7.47 us
    mul x3, other arithmetic, rate_rows(): jumps = (nearby - fields[None, :, :]) * face_areas[:, :, None]  6.95 us
    dot_general x3, matrix products, rate_rows(): jnp.einsum('kvw,kcwn->cvn', mixing, jumps, precision=lax.Precision.HIGHEST)  6.11 us
  transfers between devices with their start and end apart: 11, of which 8 were waited for; matrix products, arithmetic and copies ran while one was open for 1% of the time, Pallas kernels for 0%

commit v1 on v0

v1 whole, which is shorter than its diff:
```python
import functools

import jax
import jax.numpy as jnp
import numpy as np
from jax import lax
from jax.experimental import pallas as pl
from jax.experimental.pallas import tpu as pltpu
from jax.sharding import PartitionSpec as P

NV = 5
NI = 9
AXIAL = 128
RAD = 4
LAYERS = 4
RIM = 512
CELLS = 2048
EXT = CELLS + 2 * RIM
ROWS = 48
SPLIT = 2 * ROWS
TILE = 256
TILES = CELLS // TILE
NEAR = 7
GROUP = 16
SOURCES = 8

SEGMENT_COEFS = (0.6, 0.6, 1.0)
MESH = pl.DeviceIdType.MESH
F32 = jnp.float32
BF16 = jnp.bfloat16


def spectral_rows():
    offsets = np.arange(NI)[:, None] - np.arange(NI)[None, :]
    sine = np.where(offsets == 0, 1.0, np.sin(np.pi * offsets / NI))
    matrix = np.where(offsets == 0, 0.0, 0.5 * np.where(offsets % 2 == 0, 1.0, -1.0) / sine)
    place = np.array([[v * 8 + n if n < 8 else NV * 8 + v for n in range(NI)] for v in range(NV)])
    full = np.zeros((ROWS, ROWS), np.float32)
    for v in range(NV):
        full[np.ix_(place[v], place[v])] = matrix
    high = full.astype(BF16)
    low = (full - high.astype(np.float32)).astype(BF16)
    return np.concatenate([np.concatenate([high, high], 1), np.concatenate([low, low], 1)], 0)


def halves(x):
    high = x.astype(BF16)
    return high, (x - high.astype(F32)).astype(BF16)


def one_hot(low):
    hit = lax.broadcasted_iota(jnp.int32, (TILE, TILE), 0) == low
    return jnp.where(hit, 1.0, 0.0).astype(BF16)


def pick(table, hot, sets, count):
    found = jnp.dot(table, hot, preferred_element_type=F32)
    sets = jnp.broadcast_to(sets, (8, TILE))
    masks = [sets == s for s in range(1, count)]
    rows = []
    for r in range(0, ROWS, 8):
        parts = []
        for base in (r, ROWS + r):
            value = found[base : base + 8]
            for s in range(1, count):
                value = jnp.where(masks[s - 1], found[s * SPLIT + base : s * SPLIT + base + 8], value)
            parts.append(value)
        rows.append(parts[0] + parts[1])
    return rows


def kernel(
    coarse, send, fsrc, weight, nbr, area, dt, mix, freq, dmat, out,
    outg, recv1, send2, recv2, rtab, ohs, ohn, near, sidn, sids, field, halo, radial, mixcol,
    ssem1, rsem1, ssem2, rsem2, hssem, hrsem,
):
    t = lax.axis_index("theta")
    i = lax.axis_index("inst")
    count = 128
    g = t // 8
    h = (t % 8) * 2 + i

    def in_phase1(s):
        return ((g + s) % GROUP) * 8 + t % 8, i

    def in_phase2(s):
        other = (h + s) % GROUP
        return g * 8 + other // 2, other % 2

    ahead = ((t + 1) % count, i)
    behind = ((t + count - 1) % count, i)
    partner = (t, 1 - i)

    barrier = pltpu.get_barrier_semaphore()
    for s in range(1, GROUP):
        pl.semaphore_signal(barrier, inc=1, device_id=in_phase1(s), device_id_type=MESH)
        pl.semaphore_signal(barrier, inc=1, device_id=in_phase2(s), device_id_type=MESH)
    pl.semaphore_signal(barrier, inc=1, device_id=ahead, device_id_type=MESH)
    pl.semaphore_signal(barrier, inc=1, device_id=behind, device_id_type=MESH)

    rows = jnp.concatenate(
        [coarse[v, 0:8, :] for v in range(NV)]
        + [coarse[v, 8:9, :] for v in range(NV)]
        + [jnp.zeros((ROWS - NV * NI, TILE), F32)],
        axis=0,
    )
    table = jnp.concatenate(halves(rows), axis=0)

    def gather_out(c, carry):
        low = jnp.maximum(send[:, pl.ds(pl.multiple_of(c * TILE, TILE), TILE)], 0)
        found = jnp.dot(table, one_hot(low), preferred_element_type=F32)
        found = found[:ROWS] + found[ROWS:]
        outg[2 * c] = found[:, :128]
        outg[2 * c + 1] = found[:, 128:]
        return carry

    lax.fori_loop(0, TILES, gather_out, 0)

    pl.semaphore_wait(barrier, 2 * (GROUP - 1) + 2)

    def phase1(s):
        return pltpu.make_async_remote_copy(
            src_ref=outg.at[(g + s) % GROUP],
            dst_ref=recv1.at[g],
            send_sem=ssem1.at[s],
            recv_sem=rsem1.at[s],
            device_id=in_phase1(s),
            device_id_type=MESH,
        )

    def phase2(s):
        return pltpu.make_async_remote_copy(
            src_ref=send2.at[(h + s) % GROUP],
            dst_ref=recv2.at[h],
            send_sem=ssem2.at[s],
            recv_sem=rsem2.at[s],
            device_id=in_phase2(s),
            device_id_type=MESH,
        )

    for s in range(1, GROUP):
        phase1(s).start()
    recv1[g] = outg[g]

    slots = fsrc[...]
    places = ((slots >> 3) & 15) * 128 + (slots >> 7) * 8 + (slots & 7)
    sids[...] = places >> 8
    links = nbr[...]
    layer = lax.broadcasted_iota(jnp.int32, (6, CELLS), 1) >> 9
    sidn[...] = jnp.where(links >= EXT, NEAR - 1, (links >> 8) - 2 * layer)

    def hot_start(c, carry):
        cells = pl.ds(pl.multiple_of(c * TILE, TILE), TILE)
        for side in range(2):
            q = fsrc[side : side + 1, cells]
            ohs[side, c] = one_hot((((q >> 3) & 1) * 128) + (q >> 7) * 8 + (q & 7))
        for k in range(6):
            ohn[k, c] = one_hot(nbr[k : k + 1, cells] & 255)
        return carry

    lax.fori_loop(0, TILES, hot_start, 0)
    sub = lax.broadcasted_iota(jnp.int32, (8, 128), 0)
    for k in range(6):
        for w in range(NV):
            column = jnp.zeros((8, 128), F32)
            for v in range(NV):
                column = jnp.where(sub == v, mix[k, v, w], column)
            mixcol[k, w] = column

    for s in range(1, GROUP):
        phase1(s).wait_recv()

    lane = lax.broadcasted_iota(jnp.int32, (8, 128), 1)

    def turn(r, carry):
        part = pl.ds(pl.multiple_of(r * 8, 8), 8)
        x = [recv1[j, part, :] for j in range(GROUP)]
        for bit in range(4):
            step = 8 << bit
            keep = (lane & step) == 0
            for a in range(GROUP):
                b = a | (1 << bit)
                if a != b:
                    low = jnp.where(keep, x[a], pltpu.roll(x[b], step, 1))
                    high = jnp.where(keep, pltpu.roll(x[a], 128 - step, 1), x[b])
                    x[a], x[b] = low, high
        for j in range(GROUP):
            send2[j, part, :] = x[j]
        return carry

    lax.fori_loop(0, ROWS // 8, turn, 0)

    for s in range(1, GROUP):
        phase2(s).start()
    recv2[h] = send2[h]
    for s in range(1, GROUP):
        phase2(s).wait_recv()

    for s in range(SOURCES):
        for side in range(2):
            high, low = halves(recv2[2 * s + side])
            rtab[s * SPLIT : s * SPLIT + ROWS, side * 128 : side * 128 + 128] = high
            rtab[s * SPLIT + ROWS : (s + 1) * SPLIT, side * 128 : side * 128 + 128] = low

    def start_tile(c, carry):
        cells = pl.ds(pl.multiple_of(c * TILE, TILE), TILE)
        first = pick(rtab[...], ohs[0, c], sids[0:1, cells], SOURCES)
        second = pick(rtab[...], ohs[1, c], sids[1:2, cells], SOURCES)
        share = jnp.broadcast_to(weight[:, cells], (8, TILE))
        for r in range(ROWS // 8):
            field[0, 8 * r : 8 * r + 8, cells] = share * first[r] + (1.0 - share) * second[r]
        return carry

    lax.fori_loop(0, TILES, start_tile, 0)

    my_row = jnp.where(i == 0, RAD - 1, 0) * AXIAL

    def exchanges(seg):
        copies = [
            pltpu.make_async_remote_copy(
                src_ref=field.at[seg, :, pl.ds((LAYERS - 1) * RIM, RIM)],
                dst_ref=halo.at[seg, 0],
                send_sem=hssem.at[seg, 0],
                recv_sem=hrsem.at[seg, 0],
                device_id=ahead,
                device_id_type=MESH,
            ),
            pltpu.make_async_remote_copy(
                src_ref=field.at[seg, :, pl.ds(0, RIM)],
                dst_ref=halo.at[seg, 1],
                send_sem=hssem.at[seg, 1],
                recv_sem=hrsem.at[seg, 1],
                device_id=behind,
                device_id_type=MESH,
            ),
        ]
        for a in range(LAYERS):
            copies.append(
                pltpu.make_async_remote_copy(
                    src_ref=field.at[seg, :, pl.ds(pl.multiple_of(a * RIM + my_row, AXIAL), AXIAL)],
                    dst_ref=radial.at[seg, :, pl.ds(a * AXIAL, AXIAL)],
                    send_sem=hssem.at[seg, 2 + a],
                    recv_sem=hrsem.at[seg, 2 + a],
                    device_id=partner,
                    device_id_type=MESH,
                )
            )
        return copies

    def put(layer_at, half, values):
        high, low = halves(values)
        for a in range(max(layer_at - 1, 0), min(layer_at + 2, LAYERS)):
            base = (2 * (layer_at - a + 1) + half) * SPLIT
            near[a, base : base + ROWS, :] = high
            near[a, base + ROWS : base + SPLIT, :] = low

    omega = freq[0]
    for seg in range(3):
        copies = exchanges(seg)
        for copy in copies:
            copy.start()
        for a in range(LAYERS):
            for half in range(2):
                put(a, half, field[seg, :, a * RIM + half * TILE : a * RIM + (half + 1) * TILE])
        for copy in copies:
            copy.wait_recv()
        for half in range(2):
            put(-1, half, halo[seg, 0, :, half * TILE : (half + 1) * TILE])
            put(LAYERS, half, halo[seg, 1, :, half * TILE : (half + 1) * TILE])
            high, low = halves(radial[seg, :, half * TILE : (half + 1) * TILE])
            base = (NEAR - 1) * SPLIT
            for a in (2 * half, 2 * half + 1):
                near[a, base : base + ROWS, :] = high
                near[a, base + ROWS : base + SPLIT, :] = low

        def rate_tile(c, carry):
            cells = pl.ds(pl.multiple_of(c * TILE, TILE), TILE)
            a = c // 2
            own = [field[seg, 8 * r : 8 * r + 8, cells] for r in range(ROWS // 8)]
            mine = near[a, pl.ds(pl.multiple_of((2 + c % 2) * SPLIT, SPLIT), SPLIT), :]
            turned = jnp.dot(dmat[...], mine, preferred_element_type=F32)
            rate = [omega * (turned[8 * r : 8 * r + 8] + turned[ROWS + 8 * r : ROWS + 8 * r + 8]) for r in range(ROWS // 8)]
            for k in range(6):
                found = pick(near[a], ohn[k, c], sidn[k : k + 1, cells], NEAR)
                face = jnp.broadcast_to(area[k : k + 1, cells], (8, TILE))
                jump = [(found[r] - own[r]) * face for r in range(ROWS // 8)]
                for v in range(NV):
                    flux = mix[k, v, 0] * jump[0]
                    for w in range(1, NV):
                        flux = flux + mix[k, v, w] * jump[w]
                    rate[v] = rate[v] - flux
                last = jnp.zeros((8, TILE), F32)
                for w in range(NV):
                    column = mixcol[k, w]
                    last = last + jnp.concatenate([column, column], axis=1) * jnp.broadcast_to(jump[NV][w : w + 1], (8, TILE))
                rate[NV] = rate[NV] - last
            step = jnp.broadcast_to(SEGMENT_COEFS[seg] * dt[:, cells], (8, TILE))
            for r in range(ROWS // 8):
                after = field[0, 8 * r : 8 * r + 8, cells] - step * rate[r]
                if seg < 2:
                    field[seg + 1, 8 * r : 8 * r + 8, cells] = after
                elif r < NV:
                    out[r, 0:8, cells] = after
                else:
                    for v in range(NV):
                        out[v, 8:9, cells] = after[v : v + 1]
            return carry

        lax.fori_loop(0, TILES, rate_tile, 0)

    for s in range(1, GROUP):
        phase1(s).wait_send()
        phase2(s).wait_send()
    for seg in range(3):
        for copy in exchanges(seg):
            copy.wait_send()


def per_device(coarse_state, send_cells, fine_source, weight, neighbours, face_area, time_step, mixing, frequency):
    vmem = pl.BlockSpec(memory_space=pltpu.VMEM)
    smem = pl.BlockSpec(memory_space=pltpu.SMEM)
    return pl.pallas_call(
        kernel,
        out_shape=jax.ShapeDtypeStruct((NV, NI, CELLS), F32),
        in_specs=[vmem] * 7 + [smem, smem, vmem],
        out_specs=vmem,
        scratch_shapes=[
            pltpu.VMEM((GROUP, ROWS, 128), F32),
            pltpu.VMEM((GROUP, ROWS, 128), F32),
            pltpu.VMEM((GROUP, ROWS, 128), F32),
            pltpu.VMEM((GROUP, ROWS, 128), F32),
            pltpu.VMEM((SOURCES * SPLIT, TILE), BF16),
            pltpu.VMEM((2, TILES, TILE, TILE), BF16),
            pltpu.VMEM((6, TILES, TILE, TILE), BF16),
            pltpu.VMEM((LAYERS, NEAR * SPLIT, TILE), BF16),
            pltpu.VMEM((6, CELLS), jnp.int32),
            pltpu.VMEM((2, CELLS), jnp.int32),
            pltpu.VMEM((3, ROWS, CELLS), F32),
            pltpu.VMEM((3, 2, ROWS, RIM), F32),
            pltpu.VMEM((3, ROWS, RIM), F32),
            pltpu.VMEM((6, NV, 8, 128), F32),
            pltpu.SemaphoreType.DMA((GROUP,)),
            pltpu.SemaphoreType.DMA((GROUP,)),
            pltpu.SemaphoreType.DMA((GROUP,)),
            pltpu.SemaphoreType.DMA((GROUP,)),
            pltpu.SemaphoreType.DMA((3, 6)),
            pltpu.SemaphoreType.DMA((3, 6)),
        ],
        compiler_params=pltpu.CompilerParams(
            collective_id=0, has_side_effects=True, vmem_limit_bytes=40 * 2**20
        ),
        name="grid_sequence",
    )(
        coarse_state,
        send_cells,
        fine_source,
        weight.reshape(1, CELLS),
        neighbours,
        face_area,
        time_step.reshape(1, CELLS),
        mixing,
        frequency,
        jnp.asarray(spectral_rows()),
    )


def solution(mesh):
    placed = (
        P(None, None, ("theta", "inst")),
        P(("theta", "inst"), None),
        P(None, ("theta", "inst")),
        P(("theta", "inst")),
        P(None, ("theta", "inst")),
        P(None, ("theta", "inst")),
        P(("theta", "inst")),
        P(),
        P(),
    )
    return jax.shard_map(
        per_device,
        mesh=mesh,
        in_specs=placed,
        out_specs=P(None, None, ("theta", "inst")),
        check_vma=False,
    )
```

time: 279 us -> 74.8 us (0.27); the launches traced: 275 us -> 74.6 us
  local copies, waits for them, and re-layouts: 175 us -> 2.77 us
  Pallas kernels: 0 us -> 71 us
  waiting for transfers between devices: 37.3 us -> 0 us
  starting transfers between devices: 33.2 us -> 0 us
  other arithmetic: 19.1 us -> 0 us
  matrix products: 8.86 us -> 0 us
    gather x9 -> x0, local copies, waits for them, and re-layouts: 159 us -> none  [the longest x6 142 us: rate_rows(): nearby = jnp.take(extended, nbr_links, axis=0)]
    pallas_call x0 -> x1, Pallas kernels: none -> 71 us  [per_device(): pl.pallas_call(kernel, out_shape=jax.ShapeDtypeStruct((NV, NI, CELLS), F3...]
    all_to_all x2 -> x0, waiting for transfers between devices: 24.5 us -> none  [the longest x1 15.9 us: per_device(): lax.all_to_all(outgoing, 'theta', split_axis=1, concat_axis=1, tiled=True)]
    all_to_all x2 -> x0, starting transfers between devices: 17.5 us -> none  [the longest x1 14 us: per_device(): lax.all_to_all(outgoing, 'theta', split_axis=1, concat_axis=1, tiled=True)]
    ppermute x9 -> x0, starting transfers between devices: 15.7 us -> none  [the longest x3 11.6 us: extended_2(): lax.ppermute(head, axis, [((i + 1) % count, i) for i in range(count)])]
    ppermute x9 -> x0, waiting for transfers between devices: 12.7 us -> none  [the longest x3 7.47 us: extended_2(): lax.ppermute(tail, axis, [(i, (i + 1) % count) for i in range(count)])]
    dot_general x6 -> x0, matrix products: 8.86 us -> none  [the longest x3 6.11 us: rate_rows(): jnp.einsum('kvw,kcwn->cvn', mixing, jumps, precision=lax.Precision.HIGHEST)]
    mul x4 -> x0, other arithmetic: 6.95 us -> none  [the longest x3 6.95 us: rate_rows(): jumps = (nearby - fields[None, :, :]) * face_areas[:, :, None]]
  transfers between devices with their start and end apart: 11 -> 0, of which waited for: 8 -> 0; matrix products, arithmetic and copies ran while one was open for 1% -> 0% of each run, Pallas kernels for 0% -> 0%
where the time goes in v1:
time: 74.8 us; the launch traced here: 74.6 us
  Pallas kernels  71 us (95%)
  local copies, waits for them, and re-layouts  2.77 us (4%)
  between operations  0.76 us (1%)
    pallas_call x1, Pallas kernels, per_device(): pl.pallas_call(kernel, out_shape=jax.ShapeDtypeStruct((NV, NI, CELLS), F3...  71 us
    unnamed x16, local copies, waits for them, and re-layouts  1.73 us

profile of v1, /device:TPU:2, one launch (start us, length us, event | category | flops | bytes accessed | tf_op | source)
XLA Modules:
  0.0 74.6 jit_solution(234339180913998423)
XLA Ops:
  0.7 0.0 copy-start.3
  0.7 0.0 copy-start.4
  0.7 0.0 copy-start.5
  0.7 0.0 copy-start.6
  0.7 0.8 %copy.12.mix = f32[6,5,5]{2,1,0:T(8,128)S(1)} copy(f32[6,5,5]{2,0,1:T(8,128)} %param.17) | data formatting | bytes 1200 | tf_op args[7]
  1.4 0.0 copy-start
  1.5 0.0 copy-start.1
  1.5 0.0 copy-start.2
  1.5 0.9 %copy.11.coarse = f32[5,9,256]{2,1,0:T(8,128)S(1)} copy(f32[5,9,256]{2,0,1:T(8,128)} %param.10) | data formatting | bytes 92160 | tf_op args[0]
  2.4 0.0 copy-done.3
  2.4 0.0 copy-done.4
  2.4 0.0 copy-done.5
  2.4 0.0 copy-done.6
  2.4 0.0 copy-done
  2.5 0.0 copy-done.1
  2.5 0.0 copy-done.2
  2.5 71.0 %grid_sequence.1 = f32[5,9,2048]{2,1,0:T(8,128)S(1)} custom-call(f32[5,9,256]{2,1,0:T(8,128)S(1)} %copy.11.coarse, s32[1,2048]{1,0:T(1,128)S(1)} %copy-done.4, s32[2,2048]{1,0:T(2,128)S(1)} %copy-done.3, f32[1,2048]{1,0:T(1,128)S(1)} %bitcast.2, s32[6,2048]{1,0:T(8,128)S(1)} %copy-done, f32[6,2048]{1,0:T(8,128)S(1)} %copy-done.1, f32[1,2048]{1,0:T(1,128)S(1)} %bitcast.3, ...), custom_call_target="tpu_custom_call" | custom-call | tf_op jit(solution)/shard_map/grid_sequence/pallas_call | solution.py:322
  73.5 1.0 %copy.13 = f32[5,9,2048]{2,0,1:T(8,128)} copy(f32[5,9,2048]{2,1,0:T(8,128)S(1)} %grid_sequence.1) | data formatting | bytes 737280 | tf_op jit(solution)/shard_map/grid_sequence/pallas_call | solution.py:322
Async XLA Ops:
  0.7 1.8 %copy-start.3 = (s32[2,2048]{1,0:T(2,128)S(1)}, s32[2,2048]{1,0:T(2,128)}, u32[]{:S(2)}) copy-start(s32[2,2048]{1,0:T(2,128)} %fsrc.1) | copy-start | bytes 49156
  0.7 1.8 %copy-start.4 = (s32[1,2048]{1,0:T(1,128)S(1)}, s32[1,2048]{1,0:T(1,128)}, u32[]{:S(2)}) copy-start(s32[1,2048]{1,0:T(1,128)} %send.1) | copy-start | bytes 24580
  0.7 1.8 %copy-start.5 = (f32[2048]{0:T(1024)S(1)}, f32[2048]{0:T(1024)}, u32[]{:S(2)}) copy-start(f32[2048]{0:T(1024)} %param.13) | copy-start | bytes 24580
  0.7 1.8 %copy-start.6 = (f32[2048]{0:T(1024)S(1)}, f32[2048]{0:T(1024)}, u32[]{:S(2)}) copy-start(f32[2048]{0:T(1024)} %param.16) | copy-start | bytes 24580
  1.4 1.0 %copy-start = (s32[6,2048]{1,0:T(8,128)S(1)}, s32[6,2048]{1,0:T(8,128)}, u32[]{:S(2)}) copy-start(s32[6,2048]{1,0:T(8,128)} %nbr.1) | copy-start | bytes 147460
  1.5 1.0 %copy-start.1 = (f32[6,2048]{1,0:T(8,128)S(1)}, f32[6,2048]{1,0:T(8,128)}, u32[]{:S(2)}) copy-start(f32[6,2048]{1,0:T(8,128)} %area.1) | copy-start | bytes 147460
  1.5 1.0 %copy-start.2 = (bf16[96,96]{1,0:T(8,128)(2,1)S(1)}, bf16[96,96]{1,0:T(8,128)(2,1)}, u32[]{:S(2)}) copy-start(bf16[96,96]{1,0:T(8,128)(2,1)} %constant.2.clone.dmat) | copy-start | bytes 55300

commit v2 on v1

--- a/solution.py
+++ b/solution.py
@@ -71,7 +71,7 @@
 
 def kernel(
     coarse, send, fsrc, weight, nbr, area, dt, mix, freq, dmat, out,
-    outg, recv1, send2, recv2, rtab, ohs, ohn, near, sidn, sids, field, halo, radial, mixcol,
+    outg, recv1, send2, recv2, rtab, ohs, ohn, near, sidn, sids, field, mixcol,
     ssem1, rsem1, ssem2, rsem2, hssem, hrsem,
 ):
     t = lax.axis_index("theta")
@@ -99,10 +99,7 @@
     pl.semaphore_signal(barrier, inc=1, device_id=behind, device_id_type=MESH)
 
     rows = jnp.concatenate(
-        [coarse[v, 0:8, :] for v in range(NV)]
-        + [coarse[v, 8:9, :] for v in range(NV)]
-        + [jnp.zeros((ROWS - NV * NI, TILE), F32)],
-        axis=0,
+        [coarse[0:8, v, :] for v in range(NV)] + [coarse[8], jnp.zeros((ROWS - NV * NI, TILE), F32)], axis=0
     )
     table = jnp.concatenate(halves(rows), axis=0)
 
@@ -159,12 +156,13 @@
         return carry
 
     lax.fori_loop(0, TILES, hot_start, 0)
+    near[:, 12 * SPLIT :, :] = jnp.zeros((2, 2 * SPLIT, TILE), BF16)
     sub = lax.broadcasted_iota(jnp.int32, (8, 128), 0)
     for k in range(6):
         for w in range(NV):
             column = jnp.zeros((8, 128), F32)
             for v in range(NV):
-                column = jnp.where(sub == v, mix[k, v, w], column)
+                column = jnp.where(sub == v, mix[v, k, w], column)
             mixcol[k, w] = column
 
     for s in range(1, GROUP):
@@ -202,126 +200,170 @@
             rtab[s * SPLIT : s * SPLIT + ROWS, side * 128 : side * 128 + 128] = high
             rtab[s * SPLIT + ROWS : (s + 1) * SPLIT, side * 128 : side * 128 + 128] = low
 
-    def start_tile(c, carry):
-        cells = pl.ds(pl.multiple_of(c * TILE, TILE), TILE)
-        first = pick(rtab[...], ohs[0, c], sids[0:1, cells], SOURCES)
-        second = pick(rtab[...], ohs[1, c], sids[1:2, cells], SOURCES)
-        share = jnp.broadcast_to(weight[:, cells], (8, TILE))
-        for r in range(ROWS // 8):
-            field[0, 8 * r : 8 * r + 8, cells] = share * first[r] + (1.0 - share) * second[r]
+    my_row = jnp.where(i == 0, RAD - 1, 0) * AXIAL
+
+    def lanes(start, size):
+        return pl.ds(pl.multiple_of(start, 128), size)
+
+    def radial_copy(seg, a):
+        return pltpu.make_async_remote_copy(
+            src_ref=field.at[seg, :, lanes(RIM + a * RIM + my_row, AXIAL)],
+            dst_ref=field.at[seg, :, lanes(EXT + a * AXIAL, AXIAL)],
+            send_sem=hssem.at[seg, a],
+            recv_sem=hrsem.at[seg, a],
+            device_id=partner,
+            device_id_type=MESH,
+        )
+
+    def behind_copy(seg):
+        return pltpu.make_async_remote_copy(
+            src_ref=field.at[seg, :, pl.ds(RIM, RIM)],
+            dst_ref=field.at[seg, :, pl.ds(RIM + CELLS, RIM)],
+            send_sem=hssem.at[seg, 4],
+            recv_sem=hrsem.at[seg, 4],
+            device_id=behind,
+            device_id_type=MESH,
+        )
+
+    def ahead_copy(seg):
+        return pltpu.make_async_remote_copy(
+            src_ref=field.at[seg, :, pl.ds(CELLS, RIM)],
+            dst_ref=field.at[seg, :, pl.ds(0, RIM)],
+            send_sem=hssem.at[seg, 5],
+            recv_sem=hrsem.at[seg, 5],
+            device_id=ahead,
+            device_id_type=MESH,
+        )
+
+    def send_layer(seg, j, a):
+        radial_copy(seg, a).start()
+
+        @pl.when(j == 0)
+        def _():
+            behind_copy(seg).start()
+
+        @pl.when(j == 1)
+        def _():
+            ahead_copy(seg).start()
+
+    def put(side, at, values):
+        high, low = halves(jnp.concatenate(values, axis=0))
+        near[side, pl.ds(pl.multiple_of(at * SPLIT, 16), ROWS), :] = high
+        near[side, pl.ds(pl.multiple_of(at * SPLIT + ROWS, 16), ROWS), :] = low
+
+    def layer_of(j):
+        return jnp.where(j == 0, 0, jnp.where(j == 1, LAYERS - 1, j - 1))
+
+    def start_layer(j, carry):
+        a = layer_of(j)
+        for half in range(2):
+            c = 2 * a + half
+            cells = lanes(c * TILE, TILE)
+            first = pick(rtab[...], ohs[0, c], sids[0:1, cells], SOURCES)
+            second = pick(rtab[...], ohs[1, c], sids[1:2, cells], SOURCES)
+            share = jnp.broadcast_to(weight[:, cells], (8, TILE))
+            begin = [share * x + (1.0 - share) * y for x, y in zip(first, second)]
+            for r in range(ROWS // 8):
+                field[0, 8 * r : 8 * r + 8, lanes(RIM + c * TILE, TILE)] = begin[r]
+            put(0, 2 + c, begin)
+        send_layer(0, j, a)
         return carry
 
-    lax.fori_loop(0, TILES, start_tile, 0)
-
-    my_row = jnp.where(i == 0, RAD - 1, 0) * AXIAL
-
-    def exchanges(seg):
-        copies = [
-            pltpu.make_async_remote_copy(
-                src_ref=field.at[seg, :, pl.ds((LAYERS - 1) * RIM, RIM)],
-                dst_ref=halo.at[seg, 0],
-                send_sem=hssem.at[seg, 0],
-                recv_sem=hrsem.at[seg, 0],
-                device_id=ahead,
-                device_id_type=MESH,
-            ),
-            pltpu.make_async_remote_copy(
-                src_ref=field.at[seg, :, pl.ds(0, RIM)],
-                dst_ref=halo.at[seg, 1],
-                send_sem=hssem.at[seg, 1],
-                recv_sem=hrsem.at[seg, 1],
-                device_id=behind,
-                device_id_type=MESH,
-            ),
-        ]
-        for a in range(LAYERS):
-            copies.append(
-                pltpu.make_async_remote_copy(
-                    src_ref=field.at[seg, :, pl.ds(pl.multiple_of(a * RIM + my_row, AXIAL), AXIAL)],
-                    dst_ref=radial.at[seg, :, pl.ds(a * AXIAL, AXIAL)],
-                    send_sem=hssem.at[seg, 2 + a],
-                    recv_sem=hrsem.at[seg, 2 + a],
-                    device_id=partner,
-                    device_id_type=MESH,
-                )
-            )
-        return copies
-
-    def put(layer_at, half, values):
-        high, low = halves(values)
-        for a in range(max(layer_at - 1, 0), min(layer_at + 2, LAYERS)):
-            base = (2 * (layer_at - a + 1) + half) * SPLIT
-            near[a, base : base + ROWS, :] = high
-            near[a, base + ROWS : base + SPLIT, :] = low
+    lax.fori_loop(0, LAYERS, start_layer, 0)
 
     omega = freq[0]
-    for seg in range(3):
-        copies = exchanges(seg)
-        for copy in copies:
-            copy.start()
-        for a in range(LAYERS):
+
+    def rate_layer(at, carry):
+        seg = at // LAYERS
+        side = seg % 2
+        j = at % LAYERS
+        a = layer_of(j)
+
+        def arrived(start, at_set):
             for half in range(2):
-                put(a, half, field[seg, :, a * RIM + half * TILE : a * RIM + (half + 1) * TILE])
-        for copy in copies:
-            copy.wait_recv()
+                put(side, at_set + half, [field[seg, :, start + half * TILE : start + (half + 1) * TILE]])
+
+        @pl.when(j == 0)
+        def _():
+            ahead_copy(seg).wait_recv()
+            arrived(0, 0)
+
+        @pl.when(j == 1)
+        def _():
+            behind_copy(seg).wait_recv()
+            arrived(RIM + CELLS, 10)
+
+        radial_copy(seg, a).wait_recv()
+        high, low = halves(field[seg, :, lanes(EXT + a * AXIAL, AXIAL)])
+        across = (12 + a // 2) * SPLIT
+        column = lanes(a % 2 * AXIAL, AXIAL)
+        near[side, pl.ds(pl.multiple_of(across, 16), ROWS), column] = high
+        near[side, pl.ds(pl.multiple_of(across + ROWS, 16), ROWS), column] = low
+
+        coef = jnp.where(seg == 2, SEGMENT_COEFS[2], SEGMENT_COEFS[0])
         for half in range(2):
-            put(-1, half, halo[seg, 0, :, half * TILE : (half + 1) * TILE])
-            put(LAYERS, half, halo[seg, 1, :, half * TILE : (half + 1) * TILE])
-            high, low = halves(radial[seg, :, half * TILE : (half + 1) * TILE])
-            base = (NEAR - 1) * SPLIT
-            for a in (2 * half, 2 * half + 1):
-                near[a, base : base + ROWS, :] = high
-                near[a, base + ROWS : base + SPLIT, :] = low
-
-        def rate_tile(c, carry):
-            cells = pl.ds(pl.multiple_of(c * TILE, TILE), TILE)
-            a = c // 2
-            own = [field[seg, 8 * r : 8 * r + 8, cells] for r in range(ROWS // 8)]
-            mine = near[a, pl.ds(pl.multiple_of((2 + c % 2) * SPLIT, SPLIT), SPLIT), :]
+            c = 2 * a + half
+            cells = lanes(c * TILE, TILE)
+            here = lanes(RIM + c * TILE, TILE)
+            own = [field[seg, 8 * r : 8 * r + 8, here] for r in range(ROWS // 8)]
+            mine = near[side, pl.ds(pl.multiple_of((2 + c) * SPLIT, 16), SPLIT), :]
             turned = jnp.dot(dmat[...], mine, preferred_element_type=F32)
             rate = [omega * (turned[8 * r : 8 * r + 8] + turned[ROWS + 8 * r : ROWS + 8 * r + 8]) for r in range(ROWS // 8)]
+            table = jnp.concatenate(
+                [
+                    near[side, pl.ds(pl.multiple_of(2 * a * SPLIT, 16), 6 * SPLIT), :],
+                    near[side, pl.ds(pl.multiple_of(across, 16), SPLIT), :],
+                ],
+                axis=0,
+            )
             for k in range(6):
-                found = pick(near[a], ohn[k, c], sidn[k : k + 1, cells], NEAR)
+                found = pick(table, ohn[k, c], sidn[k : k + 1, cells], NEAR)
                 face = jnp.broadcast_to(area[k : k + 1, cells], (8, TILE))
                 jump = [(found[r] - own[r]) * face for r in range(ROWS // 8)]
                 for v in range(NV):
-                    flux = mix[k, v, 0] * jump[0]
+                    flux = mix[v, k, 0] * jump[0]
                     for w in range(1, NV):
-                        flux = flux + mix[k, v, w] * jump[w]
+                        flux = flux + mix[v, k, w] * jump[w]
                     rate[v] = rate[v] - flux
                 last = jnp.zeros((8, TILE), F32)
                 for w in range(NV):
                     column = mixcol[k, w]
                     last = last + jnp.concatenate([column, column], axis=1) * jnp.broadcast_to(jump[NV][w : w + 1], (8, TILE))
                 rate[NV] = rate[NV] - last
-            step = jnp.broadcast_to(SEGMENT_COEFS[seg] * dt[:, cells], (8, TILE))
+            step = jnp.broadcast_to(coef * dt[:, cells], (8, TILE))
+            after = [field[0, 8 * r : 8 * r + 8, here] - step * rate[r] for r in range(ROWS // 8)]
             for r in range(ROWS // 8):
-                after = field[0, 8 * r : 8 * r + 8, cells] - step * rate[r]
-                if seg < 2:
-                    field[seg + 1, 8 * r : 8 * r + 8, cells] = after
-                elif r < NV:
-                    out[r, 0:8, cells] = after
-                else:
-                    for v in range(NV):
-                        out[v, 8:9, cells] = after[v : v + 1]
-            return carry
-
-        lax.fori_loop(0, TILES, rate_tile, 0)
+                field[seg + 1, 8 * r : 8 * r + 8, here] = after[r]
+            put(1 - side, 2 + c, after)
+
+        @pl.when(seg < 2)
+        def _():
+            send_layer(seg + 1, j, a)
+
+        return carry
+
+    lax.fori_loop(0, 3 * LAYERS, rate_layer, 0)
+
+    for v in range(NV):
+        out[0:8, v, :] = field[3, 8 * v : 8 * v + 8, RIM : RIM + CELLS]
+    out[8] = field[3, 8 * NV : 9 * NV, RIM : RIM + CELLS]
 
     for s in range(1, GROUP):
         phase1(s).wait_send()
         phase2(s).wait_send()
     for seg in range(3):
-        for copy in exchanges(seg):
-            copy.wait_send()
+        for a in range(LAYERS):
+            radial_copy(seg, a).wait_send()
+        behind_copy(seg).wait_send()
+        ahead_copy(seg).wait_send()
 
 
 def per_device(coarse_state, send_cells, fine_source, weight, neighbours, face_area, time_step, mixing, frequency):
     vmem = pl.BlockSpec(memory_space=pltpu.VMEM)
     smem = pl.BlockSpec(memory_space=pltpu.SMEM)
-    return pl.pallas_call(
+    fine = pl.pallas_call(
         kernel,
-        out_shape=jax.ShapeDtypeStruct((NV, NI, CELLS), F32),
+        out_shape=jax.ShapeDtypeStruct((NI, NV, CELLS), F32),
         in_specs=[vmem] * 7 + [smem, smem, vmem],
         out_specs=vmem,
         scratch_shapes=[
@@ -332,12 +374,10 @@
             pltpu.VMEM((SOURCES * SPLIT, TILE), BF16),
             pltpu.VMEM((2, TILES, TILE, TILE), BF16),
             pltpu.VMEM((6, TILES, TILE, TILE), BF16),
-            pltpu.VMEM((LAYERS, NEAR * SPLIT, TILE), BF16),
+            pltpu.VMEM((2, 14 * SPLIT, TILE), BF16),
             pltpu.VMEM((6, CELLS), jnp.int32),
             pltpu.VMEM((2, CELLS), jnp.int32),
-            pltpu.VMEM((3, ROWS, CELLS), F32),
-            pltpu.VMEM((3, 2, ROWS, RIM), F32),
-            pltpu.VMEM((3, ROWS, RIM), F32),
+            pltpu.VMEM((4, ROWS, CELLS + 3 * RIM), F32),
             pltpu.VMEM((6, NV, 8, 128), F32),
             pltpu.SemaphoreType.DMA((GROUP,)),
             pltpu.SemaphoreType.DMA((GROUP,)),
@@ -351,17 +391,18 @@
         ),
         name="grid_sequence",
     )(
-        coarse_state,
+        coarse_state.transpose(1, 0, 2),
         send_cells,
         fine_source,
         weight.reshape(1, CELLS),
         neighbours,
         face_area,
         time_step.reshape(1, CELLS),
-        mixing,
+        mixing.transpose(1, 0, 2),
         frequency,
         jnp.asarray(spectral_rows()),
     )
+    return fine.transpose(1, 0, 2)
 
 
 def solution(mesh):

time: 74.8 us -> 66.5 us (0.89)
  Pallas kernels: 71 us -> 58.1 us
  local copies, waits for them, and re-layouts: 2.77 us -> 6.98 us
    pallas_call x1, Pallas kernels: 71 us -> 58.1 us  [per_device(): pl.pallas_call(kernel, out_shape=jax.ShapeDtypeStruct((NI, NV, CELLS), F3...]
    unnamed x16 -> x19, local copies, waits for them, and re-layouts: 1.73 us -> 6.98 us
    pallas_call x1 -> x0, local copies, waits for them, and re-layouts: 1.05 us -> none  [per_device(): pl.pallas_call(kernel, out_shape=jax.ShapeDtypeStruct((NV, NI, CELLS), F3...]
where the time goes in v2:
time: 66.5 us; the launch traced here: 65.8 us
  Pallas kernels  58.1 us (87%)
  local copies, waits for them, and re-layouts  6.98 us (10%)
  between operations  0.68 us (1%)
    pallas_call x1, Pallas kernels, per_device(): pl.pallas_call(kernel, out_shape=jax.ShapeDtypeStruct((NI, NV, CELLS), F3...  58.1 us
    unnamed x19, local copies, waits for them, and re-layouts  6.98 us

profile of v2, /device:TPU:2, one launch (start us, length us, event | category | flops | bytes accessed | tf_op | source)
XLA Modules:
  0.0 65.8 jit_solution(5718439678357773447)
XLA Ops:
  0.0 0.0 copy-start.6
  0.7 0.0 copy-done.6
  0.7 0.0 copy-start
  0.7 0.9 %copy-done = f32[5,9,256]{2,0,1:T(8,128)S(1)} copy-done((f32[5,9,256]{2,0,1:T(8,128)S(1)}, f32[5,9,256]{2,0,1:T(8,128)}, u32[]{:S(2)}) %copy-start) | copy-done | bytes 46104
  1.6 0.0 copy-start.1
  1.6 0.8 %copy-done.1 = s32[6,2048]{1,0:T(8,128)S(1)} copy-done((s32[6,2048]{1,0:T(8,128)S(1)}, s32[6,2048]{1,0:T(8,128)}, u32[]{:S(2)}) %copy-start.1) | copy-done | bytes 49176
  2.4 0.0 copy-start.2
  2.4 0.8 %copy-done.2 = f32[6,2048]{1,0:T(8,128)S(1)} copy-done((f32[6,2048]{1,0:T(8,128)S(1)}, f32[6,2048]{1,0:T(8,128)}, u32[]{:S(2)}) %copy-start.2) | copy-done | bytes 49176
  3.3 0.0 copy-start.3
  3.3 0.7 %copy-done.3 = bf16[96,96]{1,0:T(8,128)(2,1)S(1)} copy-done((bf16[96,96]{1,0:T(8,128)(2,1)S(1)}, bf16[96,96]{1,0:T(8,128)(2,1)}, u32[]{:S(2)}) %copy-start.3) | copy-done | bytes 18456
  4.0 0.0 copy-start.4
  4.0 0.7 %copy-done.4 = f32[6,5,5]{2,0,1:T(8,128)S(1)} copy-done((f32[6,5,5]{2,0,1:T(8,128)S(1)}, f32[6,5,5]{2,0,1:T(8,128)}, u32[]{:S(2)}) %copy-start.4) | copy-done | bytes 624
  4.7 0.0 copy-start.5
  4.7 0.7 %copy-done.5 = s32[2,2048]{1,0:T(2,128)S(1)} copy-done((s32[2,2048]{1,0:T(2,128)S(1)}, s32[2,2048]{1,0:T(2,128)}, u32[]{:S(2)}) %copy-start.5) | copy-done | bytes 16408
  5.4 0.0 copy-start.7
  5.4 0.7 %copy-done.7 = f32[2048]{0:T(1024)S(1)} copy-done((f32[2048]{0:T(1024)S(1)}, f32[2048]{0:T(1024)}, u32[]{:S(2)}) %copy-start.7) | copy-done | bytes 8216
  6.1 0.0 copy-start.8
  6.1 0.7 %copy-done.8 = f32[2048]{0:T(1024)S(1)} copy-done((f32[2048]{0:T(1024)S(1)}, f32[2048]{0:T(1024)}, u32[]{:S(2)}) %copy-start.8) | copy-done | bytes 8216
  6.8 58.1 %grid_sequence.1 = f32[9,5,2048]{2,1,0:T(8,128)S(1)} custom-call(f32[9,5,256]{2,1,0:T(8,128)S(1)} %bitcast.6, s32[1,2048]{1,0:T(1,128)S(1)} %copy-done.6, s32[2,2048]{1,0:T(2,128)S(1)} %copy-done.5, f32[1,2048]{1,0:T(1,128)S(1)} %bitcast.8, s32[6,2048]{1,0:T(8,128)S(1)} %copy-done.1, f32[6,2048]{1,0:T(8,128)S(1)} %copy-done.2, f32[1,2048]{1,0:T(1,128)S(1)} %bitcast.9, ...), custom_call_target="tpu_custom_call" | custom-call | tf_op jit(solution)/shard_map/grid_sequence/pallas_call | solution.py:364
  65.0 0.8 %copy.13 = f32[5,9,2048]{2,0,1:T(8,128)} copy(f32[5,9,2048]{2,0,1:T(8,128)S(1)} %bitcast.5) | data formatting | bytes 737280
Async XLA Ops:
  0.0 0.7 %copy-start.6 = (s32[1,2048]{1,0:T(1,128)S(1)}, s32[1,2048]{1,0:T(1,128)}, u32[]{:S(2)}) copy-start(s32[1,2048]{1,0:T(1,128)} %send.1) | copy-start | bytes 24580
  0.7 0.9 %copy-start = (f32[5,9,256]{2,0,1:T(8,128)S(1)}, f32[5,9,256]{2,0,1:T(8,128)}, u32[]{:S(2)}) copy-start(f32[5,9,256]{2,0,1:T(8,128)} %param.10) | copy-start | bytes 138244
  1.6 0.8 %copy-start.1 = (s32[6,2048]{1,0:T(8,128)S(1)}, s32[6,2048]{1,0:T(8,128)}, u32[]{:S(2)}) copy-start(s32[6,2048]{1,0:T(8,128)} %nbr.1) | copy-start | bytes 147460
  2.4 0.8 %copy-start.2 = (f32[6,2048]{1,0:T(8,128)S(1)}, f32[6,2048]{1,0:T(8,128)}, u32[]{:S(2)}) copy-start(f32[6,2048]{1,0:T(8,128)} %area.1) | copy-start | bytes 147460
  3.3 0.7 %copy-start.3 = (bf16[96,96]{1,0:T(8,128)(2,1)S(1)}, bf16[96,96]{1,0:T(8,128)(2,1)}, u32[]{:S(2)}) copy-start(bf16[96,96]{1,0:T(8,128)(2,1)} %constant.2.clone.dmat) | copy-start | bytes 55300
  4.0 0.7 %copy-start.4 = (f32[6,5,5]{2,0,1:T(8,128)S(1)}, f32[6,5,5]{2,0,1:T(8,128)}, u32[]{:S(2)}) copy-start(f32[6,5,5]{2,0,1:T(8,128)} %param.17) | copy-start | bytes 1804
  4.7 0.7 %copy-start.5 = (s32[2,2048]{1,0:T(2,128)S(1)}, s32[2,2048]{1,0:T(2,128)}, u32[]{:S(2)}) copy-start(s32[2,2048]{1,0:T(2,128)} %fsrc.1) | copy-start | bytes 49156
  5.4 0.7 %copy-start.7 = (f32[2048]{0:T(1024)S(1)}, f32[2048]{0:T(1024)}, u32[]{:S(2)}) copy-start(f32[2048]{0:T(1024)} %param.13) | copy-start | bytes 24580
  6.1 0.7 %copy-start.8 = (f32[2048]{0:T(1024)S(1)}, f32[2048]{0:T(1024)}, u32[]{:S(2)}) copy-start(f32[2048]{0:T(1024)} %param.16) | copy-start | bytes 24580

commit v3 on v2

--- a/solution.py
+++ b/solution.py
@@ -22,6 +22,8 @@
 TILES = CELLS // TILE
 NEAR = 7
 GROUP = 16
+CHUNK = 16
+CHUNKS = ROWS // CHUNK
 SOURCES = 8
 
 SEGMENT_COEFS = (0.6, 0.6, 1.0)
@@ -70,41 +72,72 @@
 
 
 def kernel(
-    coarse, send, fsrc, weight, nbr, area, dt, mix, freq, dmat, out,
-    outg, recv1, send2, recv2, rtab, ohs, ohn, near, sidn, sids, field, mixcol,
+    coarse_in, send_in, fsrc_in, weight_in, nbr_in, area_in, dt_in, mix_in, freq_in, dmat_in, out,
+    coarse, send, fsrc, weight, nbr, area, dt, mix, freq, dmat, isem, outg, recv1, send2, recv2, rtab, ohs, ohn, near, sidn, sids, field, mixcol,
     ssem1, rsem1, ssem2, rsem2, hssem, hrsem,
 ):
+    inputs = [
+        pltpu.make_async_copy(src, dst, isem.at[at])
+        for at, (src, dst) in enumerate(
+            [
+                (coarse_in, coarse), (send_in, send), (fsrc_in, fsrc), (nbr_in, nbr), (mix_in, mix),
+                (freq_in, freq), (weight_in, weight), (area_in, area), (dt_in, dt), (dmat_in, dmat),
+            ]
+        )
+    ]
+    for copy in inputs:
+        copy.start()
+
     t = lax.axis_index("theta")
     i = lax.axis_index("inst")
     count = 128
-    g = t // 8
-    h = (t % 8) * 2 + i
+    z, x_lo, y, core = t // 16, t // 8 % 2, t // 2 % 4, t % 2
+    g = z * 2 + core
+    h = y * 4 + x_lo * 2 + i
 
     def in_phase1(s):
-        return ((g + s) % GROUP) * 8 + t % 8, i
+        other = (g + s) % GROUP
+        return ((other // 2 * 2 + x_lo) * 4 + y) * 2 + other % 2, i
 
     def in_phase2(s):
         other = (h + s) % GROUP
-        return g * 8 + other // 2, other % 2
+        return ((z * 2 + other // 2 % 2) * 4 + other // 4) * 2 + core, other % 2
 
     ahead = ((t + 1) % count, i)
     behind = ((t + count - 1) % count, i)
     partner = (t, 1 - i)
 
+    def lanes(start, size):
+        return pl.ds(pl.multiple_of(start, 128), size)
+
     barrier = pltpu.get_barrier_semaphore()
-    for s in range(1, GROUP):
+
+    def greet(s, carry):
         pl.semaphore_signal(barrier, inc=1, device_id=in_phase1(s), device_id_type=MESH)
         pl.semaphore_signal(barrier, inc=1, device_id=in_phase2(s), device_id_type=MESH)
+        return carry
+
+    lax.fori_loop(1, GROUP, greet, 0)
     pl.semaphore_signal(barrier, inc=1, device_id=ahead, device_id_type=MESH)
     pl.semaphore_signal(barrier, inc=1, device_id=behind, device_id_type=MESH)
+
+    inputs[0].wait()
+    inputs[1].wait()
 
     rows = jnp.concatenate(
         [coarse[0:8, v, :] for v in range(NV)] + [coarse[8], jnp.zeros((ROWS - NV * NI, TILE), F32)], axis=0
     )
     table = jnp.concatenate(halves(rows), axis=0)
 
+    lane = lax.broadcasted_iota(jnp.int32, (8, 128), 1)
+
     def gather_out(c, carry):
-        low = jnp.maximum(send[:, pl.ds(pl.multiple_of(c * TILE, TILE), TILE)], 0)
+        even = send[:, lanes(c * TILE, 128)]
+        odd = send[:, lanes(c * TILE + 128, 128)]
+        keep = (lane[:1] & 16) == 0
+        first = jnp.where(keep, even, pltpu.roll(odd, 16, 1))
+        second = jnp.where(keep, pltpu.roll(even, 112, 1), odd)
+        low = jnp.maximum(jnp.concatenate([first, second], axis=1), 0)
         found = jnp.dot(table, one_hot(low), preferred_element_type=F32)
         found = found[:ROWS] + found[ROWS:]
         outg[2 * c] = found[:, :128]
@@ -115,33 +148,50 @@
 
     pl.semaphore_wait(barrier, 2 * (GROUP - 1) + 2)
 
-    def phase1(s):
+    def phase1(c, s):
+        part = pl.ds(c * CHUNK, CHUNK)
         return pltpu.make_async_remote_copy(
-            src_ref=outg.at[(g + s) % GROUP],
-            dst_ref=recv1.at[g],
-            send_sem=ssem1.at[s],
-            recv_sem=rsem1.at[s],
+            src_ref=outg.at[(g + s) % GROUP, part],
+            dst_ref=recv1.at[g, part],
+            send_sem=ssem1.at[c, s],
+            recv_sem=rsem1.at[c, s],
             device_id=in_phase1(s),
             device_id_type=MESH,
         )
 
-    def phase2(s):
+    def phase2(c, s):
+        part = pl.ds(c * CHUNK, CHUNK)
         return pltpu.make_async_remote_copy(
-            src_ref=send2.at[(h + s) % GROUP],
-            dst_ref=recv2.at[h],
-            send_sem=ssem2.at[s],
-            recv_sem=rsem2.at[s],
+            src_ref=send2.at[(h + s) % GROUP, part],
+            dst_ref=recv2.at[h, part],
+            send_sem=ssem2.at[c, s],
+            recv_sem=rsem2.at[c, s],
             device_id=in_phase2(s),
             device_id_type=MESH,
         )
 
-    for s in range(1, GROUP):
-        phase1(s).start()
+    def each(action):
+        def one(s, carry):
+            action(s)
+            return carry
+
+        lax.fori_loop(1, GROUP, one, 0)
+
+    for c in range(CHUNKS):
+        each(lambda s: phase1(c, s).start())
     recv1[g] = outg[g]
 
+    for copy in inputs[2:5]:
+        copy.wait()
+
     slots = fsrc[...]
-    places = ((slots >> 3) & 15) * 128 + (slots >> 7) * 8 + (slots & 7)
+    owner = slots >> 3
+    from_g = (owner >> 5) * 2 + ((owner >> 1) & 1)
+    from_h = ((owner >> 2) & 3) * 4 + ((owner >> 4) & 1) * 2 + (owner & 1)
+    places = from_h * 128 + from_g * 8 + (slots & 7)
+    low_places = places & 255
     sids[...] = places >> 8
+    fsrc[...] = low_places
     links = nbr[...]
     layer = lax.broadcasted_iota(jnp.int32, (6, CELLS), 1) >> 9
     sidn[...] = jnp.where(links >= EXT, NEAR - 1, (links >> 8) - 2 * layer)
@@ -149,8 +199,7 @@
     def hot_start(c, carry):
         cells = pl.ds(pl.multiple_of(c * TILE, TILE), TILE)
         for side in range(2):
-            q = fsrc[side : side + 1, cells]
-            ohs[side, c] = one_hot((((q >> 3) & 1) * 128) + (q >> 7) * 8 + (q & 7))
+            ohs[side, c] = one_hot(fsrc[side : side + 1, cells])
         for k in range(6):
             ohn[k, c] = one_hot(nbr[k : k + 1, cells] & 255)
         return carry
@@ -165,34 +214,26 @@
                 column = jnp.where(sub == v, mix[v, k, w], column)
             mixcol[k, w] = column
 
-    for s in range(1, GROUP):
-        phase1(s).wait_recv()
-
-    lane = lax.broadcasted_iota(jnp.int32, (8, 128), 1)
-
-    def turn(r, carry):
-        part = pl.ds(pl.multiple_of(r * 8, 8), 8)
-        x = [recv1[j, part, :] for j in range(GROUP)]
-        for bit in range(4):
-            step = 8 << bit
-            keep = (lane & step) == 0
-            for a in range(GROUP):
-                b = a | (1 << bit)
-                if a != b:
-                    low = jnp.where(keep, x[a], pltpu.roll(x[b], step, 1))
-                    high = jnp.where(keep, pltpu.roll(x[a], 128 - step, 1), x[b])
-                    x[a], x[b] = low, high
-        for j in range(GROUP):
-            send2[j, part, :] = x[j]
-        return carry
-
-    lax.fori_loop(0, ROWS // 8, turn, 0)
-
-    for s in range(1, GROUP):
-        phase2(s).start()
+    for c in range(CHUNKS):
+        each(lambda s: phase1(c, s).wait_recv())
+        for r in range(CHUNK // 8):
+            part = pl.ds(c * CHUNK + 8 * r, 8)
+            x = [recv1[j, part, :] for j in range(GROUP)]
+            for bit in range(4):
+                step = 8 << bit
+                keep = (lane & step) == 0
+                for a in range(GROUP):
+                    b = a | (1 << bit)
+                    if a != b:
+                        low = jnp.where(keep, x[a], pltpu.roll(x[b], step, 1))
+                        high = jnp.where(keep, pltpu.roll(x[a], 128 - step, 1), x[b])
+                        x[a], x[b] = low, high
+            for j in range(GROUP):
+                send2[j, part, :] = x[j]
+        each(lambda s: phase2(c, s).start())
     recv2[h] = send2[h]
-    for s in range(1, GROUP):
-        phase2(s).wait_recv()
+    for c in range(CHUNKS):
+        each(lambda s: phase2(c, s).wait_recv())
 
     for s in range(SOURCES):
         for side in range(2):
@@ -201,9 +242,6 @@
             rtab[s * SPLIT + ROWS : (s + 1) * SPLIT, side * 128 : side * 128 + 128] = low
 
     my_row = jnp.where(i == 0, RAD - 1, 0) * AXIAL
-
-    def lanes(start, size):
-        return pl.ds(pl.multiple_of(start, 128), size)
 
     def radial_copy(seg, a):
         return pltpu.make_async_remote_copy(
@@ -238,11 +276,11 @@
     def send_layer(seg, j, a):
         radial_copy(seg, a).start()
 
-        @pl.when(j == 0)
+        @pl.when(j == 2)
         def _():
             behind_copy(seg).start()
 
-        @pl.when(j == 1)
+        @pl.when(j == 3)
         def _():
             ahead_copy(seg).start()
 
@@ -252,7 +290,10 @@
         near[side, pl.ds(pl.multiple_of(at * SPLIT + ROWS, 16), ROWS), :] = low
 
     def layer_of(j):
-        return jnp.where(j == 0, 0, jnp.where(j == 1, LAYERS - 1, j - 1))
+        return jnp.where(j < 2, j + 1, (j - 2) * 3)
+
+    for copy in inputs[5:]:
+        copy.wait()
 
     def start_layer(j, carry):
         a = layer_of(j)
@@ -283,12 +324,12 @@
             for half in range(2):
                 put(side, at_set + half, [field[seg, :, start + half * TILE : start + (half + 1) * TILE]])
 
-        @pl.when(j == 0)
+        @pl.when(j == 2)
         def _():
             ahead_copy(seg).wait_recv()
             arrived(0, 0)
 
-        @pl.when(j == 1)
+        @pl.when(j == 3)
         def _():
             behind_copy(seg).wait_recv()
             arrived(RIM + CELLS, 10)
@@ -348,9 +389,9 @@
         out[0:8, v, :] = field[3, 8 * v : 8 * v + 8, RIM : RIM + CELLS]
     out[8] = field[3, 8 * NV : 9 * NV, RIM : RIM + CELLS]
 
-    for s in range(1, GROUP):
-        phase1(s).wait_send()
-        phase2(s).wait_send()
+    for c in range(CHUNKS):
+        each(lambda s: phase1(c, s).wait_send())
+        each(lambda s: phase2(c, s).wait_send())
     for seg in range(3):
         for a in range(LAYERS):
             radial_copy(seg, a).wait_send()
@@ -360,13 +401,24 @@
 
 def per_device(coarse_state, send_cells, fine_source, weight, neighbours, face_area, time_step, mixing, frequency):
     vmem = pl.BlockSpec(memory_space=pltpu.VMEM)
-    smem = pl.BlockSpec(memory_space=pltpu.SMEM)
+    hbm = pl.BlockSpec(memory_space=pltpu.HBM)
     fine = pl.pallas_call(
         kernel,
         out_shape=jax.ShapeDtypeStruct((NI, NV, CELLS), F32),
-        in_specs=[vmem] * 7 + [smem, smem, vmem],
+        in_specs=[hbm] * 10,
         out_specs=vmem,
         scratch_shapes=[
+            pltpu.VMEM((NI, NV, TILE), F32),
+            pltpu.VMEM((1, CELLS), jnp.int32),
+            pltpu.VMEM((2, CELLS), jnp.int32),
+            pltpu.VMEM((1, CELLS), F32),
+            pltpu.VMEM((6, CELLS), jnp.int32),
+            pltpu.VMEM((6, CELLS), F32),
+            pltpu.VMEM((1, CELLS), F32),
+            pltpu.SMEM((NV, 6, NV), F32),
+            pltpu.SMEM((1,), F32),
+            pltpu.VMEM((SPLIT, SPLIT), BF16),
+            pltpu.SemaphoreType.DMA((10,)),
             pltpu.VMEM((GROUP, ROWS, 128), F32),
             pltpu.VMEM((GROUP, ROWS, 128), F32),
             pltpu.VMEM((GROUP, ROWS, 128), F32),
@@ -379,28 +431,33 @@
             pltpu.VMEM((2, CELLS), jnp.int32),
             pltpu.VMEM((4, ROWS, CELLS + 3 * RIM), F32),
             pltpu.VMEM((6, NV, 8, 128), F32),
-            pltpu.SemaphoreType.DMA((GROUP,)),
-            pltpu.SemaphoreType.DMA((GROUP,)),
-            pltpu.SemaphoreType.DMA((GROUP,)),
-            pltpu.SemaphoreType.DMA((GROUP,)),
+            pltpu.SemaphoreType.DMA((CHUNKS, GROUP)),
+            pltpu.SemaphoreType.DMA((CHUNKS, GROUP)),
+            pltpu.SemaphoreType.DMA((CHUNKS, GROUP)),
+            pltpu.SemaphoreType.DMA((CHUNKS, GROUP)),
             pltpu.SemaphoreType.DMA((3, 6)),
             pltpu.SemaphoreType.DMA((3, 6)),
         ],
         compiler_params=pltpu.CompilerParams(
-            collective_id=0, has_side_effects=True, vmem_limit_bytes=40 * 2**20
+            collective_id=0, has_side_effects=True, vmem_limit_bytes=48 * 2**20
         ),
         name="grid_sequence",
     )(
-        coarse_state.transpose(1, 0, 2),
-        send_cells,
-        fine_source,
-        weight.reshape(1, CELLS),
-        neighbours,
-        face_area,
-        time_step.reshape(1, CELLS),
-        mixing.transpose(1, 0, 2),
-        frequency,
-        jnp.asarray(spectral_rows()),
+        *[
+            x if x.shape == (1,) else pltpu.with_memory_space_constraint(x, pltpu.HBM)
+            for x in (
+                coarse_state.transpose(1, 0, 2),
+                send_cells,
+                fine_source,
+                weight.reshape(1, CELLS),
+                neighbours,
+                face_area,
+                time_step.reshape(1, CELLS),
+                mixing.transpose(1, 0, 2),
+                frequency,
+                jnp.asarray(spectral_rows()),
+            )
+        ]
     )
     return fine.transpose(1, 0, 2)
 

time: 66.5 us -> 56.4 us (0.85)
  local copies, waits for them, and re-layouts: 6.98 us -> 0.82 us
  Pallas kernels: 58.1 us -> 54.8 us
    unnamed x19 -> x1, local copies, waits for them, and re-layouts: 6.98 us -> 0.82 us
    pallas_call x1, Pallas kernels: 58.1 us -> 54.8 us  [per_device(): pl.pallas_call(kernel, out_shape=jax.ShapeDtypeStruct((NI, NV, CELLS), F3...]
where the time goes in v3:
time: 56.4 us; the launch traced here: 56.3 us
  Pallas kernels  54.8 us (97%)
  local copies, waits for them, and re-layouts  0.82 us (1%)
  between operations  0.66 us (1%)
    pallas_call x1, Pallas kernels, per_device(): pl.pallas_call(kernel, out_shape=jax.ShapeDtypeStruct((NI, NV, CELLS), F3...  54.8 us

profile of v3, /device:TPU:2, one launch (start us, length us, event | category | flops | bytes accessed | tf_op | source)
XLA Modules:
  0.0 56.3 jit_solution(5330709581655062987)
XLA Ops:
  0.7 54.8 %grid_sequence.1 = f32[9,5,2048]{2,1,0:T(8,128)S(1)} custom-call(f32[9,5,256]{2,1,0:T(8,128)} %bitcast.6, s32[1,2048]{1,0:T(1,128)} %send_in.1, s32[2,2048]{1,0:T(2,128)} %fsrc_in.1, f32[1,2048]{1,0:T(1,128)} %bitcast.8, s32[6,2048]{1,0:T(8,128)} %nbr_in.1, f32[6,2048]{1,0:T(8,128)} %area_in.1, f32[1,2048]{1,0:T(1,128)} %bitcast.9, f32[5,6,5]{2,1,0:T(8,128)} %bitcast.7, ...), custom_call_target="tpu_custom_call" | custom-call | tf_op jit(solution)/shard_map/grid_sequence/pallas_call | solution.py:405
  55.5 0.8 %copy.13 = f32[5,9,2048]{2,0,1:T(8,128)} copy(f32[5,9,2048]{2,0,1:T(8,128)S(1)} %bitcast.5) | data formatting | bytes 737280

commit v4 on v3

--- a/solution.py
+++ b/solution.py
@@ -21,8 +21,11 @@
 TILE = 256
 TILES = CELLS // TILE
 NEAR = 7
+NEAR_BLOCKS = 13
+TOGETHER = 1
+BY_LANES = {}
 GROUP = 16
-CHUNK = 16
+CHUNK = 24
 CHUNKS = ROWS // CHUNK
 SOURCES = 8
 
@@ -71,9 +74,26 @@
     return rows
 
 
+def turn_lanes(blocks, place, sets):
+    columns = []
+    for at in range(0, TILE, 128):
+        lane = jnp.broadcast_to(place[:, at : at + 128], (8, 128))
+        block = jnp.broadcast_to(sets[:, at : at + 128], (8, 128))
+        masks = [block == s for s in range(1, NEAR_BLOCKS)]
+        rows = []
+        for r in range(ROWS // 8):
+            value = jnp.take_along_axis(blocks(0, r), lane, axis=1, mode="promise_in_bounds")
+            for s in range(1, NEAR_BLOCKS):
+                found = jnp.take_along_axis(blocks(s, r), lane, axis=1, mode="promise_in_bounds")
+                value = jnp.where(masks[s - 1], found, value)
+            rows.append(value)
+        columns.append(rows)
+    return [jnp.concatenate([x, y], axis=1) for x, y in zip(*columns)]
+
+
 def kernel(
     coarse_in, send_in, fsrc_in, weight_in, nbr_in, area_in, dt_in, mix_in, freq_in, dmat_in, out,
-    coarse, send, fsrc, weight, nbr, area, dt, mix, freq, dmat, isem, outg, recv1, send2, recv2, rtab, ohs, ohn, near, sidn, sids, field, mixcol,
+    coarse, send, fsrc, weight, nbr, area, dt, mix, freq, dmat, isem, outg, recv1, send2, recv2, rtab, ohs, ohn, near0, near1, sidn, sids, field0, field1, field2, field3, mixcol,
     ssem1, rsem1, ssem2, rsem2, hssem, hrsem,
 ):
     inputs = [
@@ -88,6 +108,8 @@
     for copy in inputs:
         copy.start()
 
+    field = [field0, field1, field2, field3]
+    near = [near0, near1]
     t = lax.axis_index("theta")
     i = lax.axis_index("inst")
     count = 128
@@ -171,11 +193,8 @@
         )
 
     def each(action):
-        def one(s, carry):
+        for s in range(1, GROUP):
             action(s)
-            return carry
-
-        lax.fori_loop(1, GROUP, one, 0)
 
     for c in range(CHUNKS):
         each(lambda s: phase1(c, s).start())
@@ -205,7 +224,8 @@
         return carry
 
     lax.fori_loop(0, TILES, hot_start, 0)
-    near[:, 12 * SPLIT :, :] = jnp.zeros((2, 2 * SPLIT, TILE), BF16)
+    for table_ref in near:
+        table_ref[12 * SPLIT :, :] = jnp.zeros((2 * SPLIT, TILE), BF16)
     sub = lax.broadcasted_iota(jnp.int32, (8, 128), 0)
     for k in range(6):
         for w in range(NV):
@@ -245,8 +265,8 @@
 
     def radial_copy(seg, a):
         return pltpu.make_async_remote_copy(
-            src_ref=field.at[seg, :, lanes(RIM + a * RIM + my_row, AXIAL)],
-            dst_ref=field.at[seg, :, lanes(EXT + a * AXIAL, AXIAL)],
+            src_ref=field[seg].at[:, lanes(RIM + a * RIM + my_row, AXIAL)],
+            dst_ref=field[seg].at[:, lanes(EXT + a * AXIAL, AXIAL)],
             send_sem=hssem.at[seg, a],
             recv_sem=hrsem.at[seg, a],
             device_id=partner,
@@ -255,8 +275,8 @@
 
     def behind_copy(seg):
         return pltpu.make_async_remote_copy(
-            src_ref=field.at[seg, :, pl.ds(RIM, RIM)],
-            dst_ref=field.at[seg, :, pl.ds(RIM + CELLS, RIM)],
+            src_ref=field[seg].at[:, pl.ds(RIM, RIM)],
+            dst_ref=field[seg].at[:, pl.ds(RIM + CELLS, RIM)],
             send_sem=hssem.at[seg, 4],
             recv_sem=hrsem.at[seg, 4],
             device_id=behind,
@@ -265,8 +285,8 @@
 
     def ahead_copy(seg):
         return pltpu.make_async_remote_copy(
-            src_ref=field.at[seg, :, pl.ds(CELLS, RIM)],
-            dst_ref=field.at[seg, :, pl.ds(0, RIM)],
+            src_ref=field[seg].at[:, pl.ds(CELLS, RIM)],
+            dst_ref=field[seg].at[:, pl.ds(0, RIM)],
             send_sem=hssem.at[seg, 5],
             recv_sem=hrsem.at[seg, 5],
             device_id=ahead,
@@ -286,8 +306,8 @@
 
     def put(side, at, values):
         high, low = halves(jnp.concatenate(values, axis=0))
-        near[side, pl.ds(pl.multiple_of(at * SPLIT, 16), ROWS), :] = high
-        near[side, pl.ds(pl.multiple_of(at * SPLIT + ROWS, 16), ROWS), :] = low
+        near[side][pl.ds(pl.multiple_of(at * SPLIT, 16), ROWS), :] = high
+        near[side][pl.ds(pl.multiple_of(at * SPLIT + ROWS, 16), ROWS), :] = low
 
     def layer_of(j):
         return jnp.where(j < 2, j + 1, (j - 2) * 3)
@@ -305,7 +325,7 @@
             share = jnp.broadcast_to(weight[:, cells], (8, TILE))
             begin = [share * x + (1.0 - share) * y for x, y in zip(first, second)]
             for r in range(ROWS // 8):
-                field[0, 8 * r : 8 * r + 8, lanes(RIM + c * TILE, TILE)] = begin[r]
+                field[0][8 * r : 8 * r + 8, lanes(RIM + c * TILE, TILE)] = begin[r]
             put(0, 2 + c, begin)
         send_layer(0, j, a)
         return carry
@@ -314,80 +334,101 @@
 
     omega = freq[0]
 
-    def rate_layer(at, carry):
-        seg = at // LAYERS
+    def rate_tile(seg, side, coef, a, half):
+        c = 2 * a + half
+        cells = lanes(c * TILE, TILE)
+        here = lanes(RIM + c * TILE, TILE)
+        across = (12 + a // 2) * SPLIT
+        own = [field[seg][8 * r : 8 * r + 8, here] for r in range(ROWS // 8)]
+        mine = near[side][pl.ds(pl.multiple_of((2 + c) * SPLIT, 16), SPLIT), :]
+        turned = jnp.dot(dmat[...], mine, preferred_element_type=F32)
+        rate = [omega * (turned[8 * r : 8 * r + 8] + turned[ROWS + 8 * r : ROWS + 8 * r + 8]) for r in range(ROWS // 8)]
+        table = jnp.concatenate(
+            [
+                near[side][pl.ds(pl.multiple_of(2 * a * SPLIT, 16), 6 * SPLIT), :],
+                near[side][pl.ds(pl.multiple_of(across, 16), SPLIT), :],
+            ],
+            axis=0,
+        )
+
+        def block(s, r):
+            start = EXT + a * AXIAL if s == NEAR_BLOCKS - 1 else a * RIM + s * 128
+            return field[seg][8 * r : 8 * r + 8, lanes(start, 128)]
+
+        for k in range(6):
+            if (half, k) in BY_LANES:
+                links = nbr[k : k + 1, cells]
+                sets = jnp.where(links >= EXT, NEAR_BLOCKS - 1, (links >> 7) - 4 * a)
+                found = turn_lanes(block, links & 127, sets)
+            else:
+                found = pick(table, ohn[k, c], sidn[k : k + 1, cells], NEAR)
+            face = jnp.broadcast_to(area[k : k + 1, cells], (8, TILE))
+            jump = [(found[r] - own[r]) * face for r in range(ROWS // 8)]
+            for v in range(NV):
+                flux = mix[v, k, 0] * jump[0]
+                for w in range(1, NV):
+                    flux = flux + mix[v, k, w] * jump[w]
+                rate[v] = rate[v] - flux
+            last = jnp.zeros((8, TILE), F32)
+            for w in range(NV):
+                column = mixcol[k, w]
+                last = last + jnp.concatenate([column, column], axis=1) * jnp.broadcast_to(jump[NV][w : w + 1], (8, TILE))
+            rate[NV] = rate[NV] - last
+        step = jnp.broadcast_to(coef * dt[:, cells], (8, TILE))
+        after = [field[0][8 * r : 8 * r + 8, here] - step * rate[r] for r in range(ROWS // 8)]
+        for r in range(ROWS // 8):
+            field[seg + 1][8 * r : 8 * r + 8, here] = after[r]
+        if seg < 2:
+            put(1 - side, 2 + c, after)
+
+    def rate_layers(seg, step_at):
         side = seg % 2
-        j = at % LAYERS
-        a = layer_of(j)
+        coef = SEGMENT_COEFS[seg]
+        group = [layer_of(step_at * TOGETHER + n) for n in range(TOGETHER)]
 
         def arrived(start, at_set):
             for half in range(2):
-                put(side, at_set + half, [field[seg, :, start + half * TILE : start + (half + 1) * TILE]])
-
-        @pl.when(j == 2)
-        def _():
-            ahead_copy(seg).wait_recv()
-            arrived(0, 0)
-
-        @pl.when(j == 3)
-        def _():
-            behind_copy(seg).wait_recv()
-            arrived(RIM + CELLS, 10)
-
-        radial_copy(seg, a).wait_recv()
-        high, low = halves(field[seg, :, lanes(EXT + a * AXIAL, AXIAL)])
-        across = (12 + a // 2) * SPLIT
-        column = lanes(a % 2 * AXIAL, AXIAL)
-        near[side, pl.ds(pl.multiple_of(across, 16), ROWS), column] = high
-        near[side, pl.ds(pl.multiple_of(across + ROWS, 16), ROWS), column] = low
-
-        coef = jnp.where(seg == 2, SEGMENT_COEFS[2], SEGMENT_COEFS[0])
-        for half in range(2):
-            c = 2 * a + half
-            cells = lanes(c * TILE, TILE)
-            here = lanes(RIM + c * TILE, TILE)
-            own = [field[seg, 8 * r : 8 * r + 8, here] for r in range(ROWS // 8)]
-            mine = near[side, pl.ds(pl.multiple_of((2 + c) * SPLIT, 16), SPLIT), :]
-            turned = jnp.dot(dmat[...], mine, preferred_element_type=F32)
-            rate = [omega * (turned[8 * r : 8 * r + 8] + turned[ROWS + 8 * r : ROWS + 8 * r + 8]) for r in range(ROWS // 8)]
-            table = jnp.concatenate(
-                [
-                    near[side, pl.ds(pl.multiple_of(2 * a * SPLIT, 16), 6 * SPLIT), :],
-                    near[side, pl.ds(pl.multiple_of(across, 16), SPLIT), :],
-                ],
-                axis=0,
-            )
-            for k in range(6):
-                found = pick(table, ohn[k, c], sidn[k : k + 1, cells], NEAR)
-                face = jnp.broadcast_to(area[k : k + 1, cells], (8, TILE))
-                jump = [(found[r] - own[r]) * face for r in range(ROWS // 8)]
-                for v in range(NV):
-                    flux = mix[v, k, 0] * jump[0]
-                    for w in range(1, NV):
-                        flux = flux + mix[v, k, w] * jump[w]
-                    rate[v] = rate[v] - flux
-                last = jnp.zeros((8, TILE), F32)
-                for w in range(NV):
-                    column = mixcol[k, w]
-                    last = last + jnp.concatenate([column, column], axis=1) * jnp.broadcast_to(jump[NV][w : w + 1], (8, TILE))
-                rate[NV] = rate[NV] - last
-            step = jnp.broadcast_to(coef * dt[:, cells], (8, TILE))
-            after = [field[0, 8 * r : 8 * r + 8, here] - step * rate[r] for r in range(ROWS // 8)]
-            for r in range(ROWS // 8):
-                field[seg + 1, 8 * r : 8 * r + 8, here] = after[r]
-            put(1 - side, 2 + c, after)
-
-        @pl.when(seg < 2)
-        def _():
-            send_layer(seg + 1, j, a)
-
-        return carry
-
-    lax.fori_loop(0, 3 * LAYERS, rate_layer, 0)
+                put(side, at_set + half, [field[seg][:, start + half * TILE : start + (half + 1) * TILE]])
+
+        for n in range(TOGETHER):
+
+            @pl.when(step_at * TOGETHER + n == 2)
+            def _():
+                ahead_copy(seg).wait_recv()
+                arrived(0, 0)
+
+            @pl.when(step_at * TOGETHER + n == 3)
+            def _():
+                behind_copy(seg).wait_recv()
+                arrived(RIM + CELLS, 10)
+
+        for a in group:
+            radial_copy(seg, a).wait_recv()
+            high, low = halves(field[seg][:, lanes(EXT + a * AXIAL, AXIAL)])
+            across = (12 + a // 2) * SPLIT
+            column = lanes(a % 2 * AXIAL, AXIAL)
+            near[side][pl.ds(pl.multiple_of(across, 16), ROWS), column] = high
+            near[side][pl.ds(pl.multiple_of(across + ROWS, 16), ROWS), column] = low
+
+        for a in group:
+            for half in range(2):
+                rate_tile(seg, side, coef, a, half)
+
+        if seg < 2:
+            for n in range(TOGETHER):
+                send_layer(seg + 1, step_at * TOGETHER + n, group[n])
+
+    for seg in range(3):
+
+        def rate_step(step_at, carry):
+            rate_layers(seg, step_at)
+            return carry
+
+        lax.fori_loop(0, LAYERS // TOGETHER, rate_step, 0)
 
     for v in range(NV):
-        out[0:8, v, :] = field[3, 8 * v : 8 * v + 8, RIM : RIM + CELLS]
-    out[8] = field[3, 8 * NV : 9 * NV, RIM : RIM + CELLS]
+        out[0:8, v, :] = field[3][8 * v : 8 * v + 8, RIM : RIM + CELLS]
+    out[8] = field[3][8 * NV : 9 * NV, RIM : RIM + CELLS]
 
     for c in range(CHUNKS):
         each(lambda s: phase1(c, s).wait_send())
@@ -426,10 +467,14 @@
             pltpu.VMEM((SOURCES * SPLIT, TILE), BF16),
             pltpu.VMEM((2, TILES, TILE, TILE), BF16),
             pltpu.VMEM((6, TILES, TILE, TILE), BF16),
-            pltpu.VMEM((2, 14 * SPLIT, TILE), BF16),
+            pltpu.VMEM((14 * SPLIT, TILE), BF16),
+            pltpu.VMEM((14 * SPLIT, TILE), BF16),
             pltpu.VMEM((6, CELLS), jnp.int32),
             pltpu.VMEM((2, CELLS), jnp.int32),
-            pltpu.VMEM((4, ROWS, CELLS + 3 * RIM), F32),
+            pltpu.VMEM((ROWS, CELLS + 3 * RIM), F32),
+            pltpu.VMEM((ROWS, CELLS + 3 * RIM), F32),
+            pltpu.VMEM((ROWS, CELLS + 3 * RIM), F32),
+            pltpu.VMEM((ROWS, CELLS + 3 * RIM), F32),
             pltpu.VMEM((6, NV, 8, 128), F32),
             pltpu.SemaphoreType.DMA((CHUNKS, GROUP)),
             pltpu.SemaphoreType.DMA((CHUNKS, GROUP)),

time: 56.4 us -> 53.4 us (0.947)
  Pallas kernels: 54.8 us -> 51.8 us
    pallas_call x1, Pallas kernels: 54.8 us -> 51.8 us  [per_device(): pl.pallas_call(kernel, out_shape=jax.ShapeDtypeStruct((NI, NV, CELLS), F3...]
where the time goes in v4:
time: 53.4 us; the launch traced here: 53.2 us
  Pallas kernels  51.8 us (97%)
  local copies, waits for them, and re-layouts  0.82 us (2%)
  between operations  0.66 us (1%)
    pallas_call x1, Pallas kernels, per_device(): pl.pallas_call(kernel, out_shape=jax.ShapeDtypeStruct((NI, NV, CELLS), F3...  51.8 us

profile of v4, /device:TPU:2, one launch (start us, length us, event | category | flops | bytes accessed | tf_op | source)
XLA Modules:
  0.0 53.2 jit_solution(16448480885545826000)
XLA Ops:
  0.7 51.8 %grid_sequence.1 = f32[9,5,2048]{2,1,0:T(8,128)S(1)} custom-call(f32[9,5,256]{2,1,0:T(8,128)} %bitcast.6, s32[1,2048]{1,0:T(1,128)} %send_in.1, s32[2,2048]{1,0:T(2,128)} %fsrc_in.1, f32[1,2048]{1,0:T(1,128)} %bitcast.8, s32[6,2048]{1,0:T(8,128)} %nbr_in.1, f32[6,2048]{1,0:T(8,128)} %area_in.1, f32[1,2048]{1,0:T(1,128)} %bitcast.9, f32[5,6,5]{2,1,0:T(8,128)} %bitcast.7, ...), custom_call_target="tpu_custom_call" | custom-call | tf_op jit(solution)/shard_map/grid_sequence/pallas_call | solution.py:446
  52.4 0.8 %copy.13 = f32[5,9,2048]{2,0,1:T(8,128)} copy(f32[5,9,2048]{2,0,1:T(8,128)S(1)} %bitcast.5) | data formatting | bytes 737280

commit v5 on v4

--- a/solution.py
+++ b/solution.py
@@ -23,7 +23,7 @@
 NEAR = 7
 NEAR_BLOCKS = 13
 TOGETHER = 1
-BY_LANES = {}
+BY_MATRIX = 5
 GROUP = 16
 CHUNK = 24
 CHUNKS = ROWS // CHUNK
@@ -45,7 +45,8 @@
         full[np.ix_(place[v], place[v])] = matrix
     high = full.astype(BF16)
     low = (full - high.astype(np.float32)).astype(BF16)
-    return np.concatenate([np.concatenate([high, high], 1), np.concatenate([low, low], 1)], 0)
+    twice = [np.concatenate([x[:, r : r + 16]] * 2, 1) for x in (high, low) for r in range(0, ROWS, 16)]
+    return np.concatenate([np.concatenate(twice[:3], 1), np.concatenate(twice[3:], 1)], 0)
 
 
 def halves(x):
@@ -65,30 +66,26 @@
     rows = []
     for r in range(0, ROWS, 8):
         parts = []
-        for base in (r, ROWS + r):
+        for half in range(2):
+            base = ((r // 16) * 2 + half) * count * 16 + r % 16
             value = found[base : base + 8]
             for s in range(1, count):
-                value = jnp.where(masks[s - 1], found[s * SPLIT + base : s * SPLIT + base + 8], value)
+                value = jnp.where(masks[s - 1], found[base + s * 16 : base + s * 16 + 8], value)
             parts.append(value)
         rows.append(parts[0] + parts[1])
     return rows
 
 
-def turn_lanes(blocks, place, sets):
-    columns = []
-    for at in range(0, TILE, 128):
-        lane = jnp.broadcast_to(place[:, at : at + 128], (8, 128))
-        block = jnp.broadcast_to(sets[:, at : at + 128], (8, 128))
-        masks = [block == s for s in range(1, NEAR_BLOCKS)]
-        rows = []
-        for r in range(ROWS // 8):
-            value = jnp.take_along_axis(blocks(0, r), lane, axis=1, mode="promise_in_bounds")
-            for s in range(1, NEAR_BLOCKS):
-                found = jnp.take_along_axis(blocks(s, r), lane, axis=1, mode="promise_in_bounds")
-                value = jnp.where(masks[s - 1], found, value)
-            rows.append(value)
-        columns.append(rows)
-    return [jnp.concatenate([x, y], axis=1) for x, y in zip(*columns)]
+def from_block(block, place, masks, values):
+    merged = []
+    for r in range(ROWS // 8):
+        rows = block(r)
+        found = [
+            jnp.take_along_axis(rows, jnp.broadcast_to(place[:, at : at + 128], (8, 128)), axis=1, mode="promise_in_bounds")
+            for at in range(0, TILE, 128)
+        ]
+        merged.append(jnp.where(masks, jnp.concatenate(found, axis=1), values[r]))
+    return merged
 
 
 def kernel(
@@ -224,8 +221,6 @@
         return carry
 
     lax.fori_loop(0, TILES, hot_start, 0)
-    for table_ref in near:
-        table_ref[12 * SPLIT :, :] = jnp.zeros((2 * SPLIT, TILE), BF16)
     sub = lax.broadcasted_iota(jnp.int32, (8, 128), 0)
     for k in range(6):
         for w in range(NV):
@@ -257,9 +252,9 @@
 
     for s in range(SOURCES):
         for side in range(2):
-            high, low = halves(recv2[2 * s + side])
-            rtab[s * SPLIT : s * SPLIT + ROWS, side * 128 : side * 128 + 128] = high
-            rtab[s * SPLIT + ROWS : (s + 1) * SPLIT, side * 128 : side * 128 + 128] = low
+            for half, values in enumerate(halves(recv2[2 * s + side])):
+                for r in range(ROWS // 16):
+                    rtab[2 * r + half, 16 * s : 16 * s + 16, side * 128 : side * 128 + 128] = values[16 * r : 16 * r + 16]
 
     my_row = jnp.where(i == 0, RAD - 1, 0) * AXIAL
 
@@ -305,9 +300,9 @@
             ahead_copy(seg).start()
 
     def put(side, at, values):
-        high, low = halves(jnp.concatenate(values, axis=0))
-        near[side][pl.ds(pl.multiple_of(at * SPLIT, 16), ROWS), :] = high
-        near[side][pl.ds(pl.multiple_of(at * SPLIT + ROWS, 16), ROWS), :] = low
+        for half, part in enumerate(halves(jnp.concatenate(values, axis=0))):
+            for r in range(ROWS // 16):
+                near[side][2 * r + half, pl.ds(pl.multiple_of(at * 16, 16), 16), :] = part[16 * r : 16 * r + 16]
 
     def layer_of(j):
         return jnp.where(j < 2, j + 1, (j - 2) * 3)
@@ -320,8 +315,8 @@
         for half in range(2):
             c = 2 * a + half
             cells = lanes(c * TILE, TILE)
-            first = pick(rtab[...], ohs[0, c], sids[0:1, cells], SOURCES)
-            second = pick(rtab[...], ohs[1, c], sids[1:2, cells], SOURCES)
+            first = pick(rtab[...].reshape(SOURCES * SPLIT, TILE), ohs[0, c], sids[0:1, cells], SOURCES)
+            second = pick(rtab[...].reshape(SOURCES * SPLIT, TILE), ohs[1, c], sids[1:2, cells], SOURCES)
             share = jnp.broadcast_to(weight[:, cells], (8, TILE))
             begin = [share * x + (1.0 - share) * y for x, y in zip(first, second)]
             for r in range(ROWS // 8):
@@ -338,30 +333,24 @@
         c = 2 * a + half
         cells = lanes(c * TILE, TILE)
         here = lanes(RIM + c * TILE, TILE)
-        across = (12 + a // 2) * SPLIT
         own = [field[seg][8 * r : 8 * r + 8, here] for r in range(ROWS // 8)]
-        mine = near[side][pl.ds(pl.multiple_of((2 + c) * SPLIT, 16), SPLIT), :]
+        mine = near[side][:, pl.ds(pl.multiple_of((2 + c) * 16, 16), 16), :].reshape(SPLIT, TILE)
         turned = jnp.dot(dmat[...], mine, preferred_element_type=F32)
         rate = [omega * (turned[8 * r : 8 * r + 8] + turned[ROWS + 8 * r : ROWS + 8 * r + 8]) for r in range(ROWS // 8)]
-        table = jnp.concatenate(
-            [
-                near[side][pl.ds(pl.multiple_of(2 * a * SPLIT, 16), 6 * SPLIT), :],
-                near[side][pl.ds(pl.multiple_of(across, 16), SPLIT), :],
-            ],
-            axis=0,
-        )
-
-        def block(s, r):
-            start = EXT + a * AXIAL if s == NEAR_BLOCKS - 1 else a * RIM + s * 128
-            return field[seg][8 * r : 8 * r + 8, lanes(start, 128)]
+        table = near[side][:, pl.ds(pl.multiple_of(2 * a * 16, 16), BY_MATRIX * 16), :].reshape(BY_MATRIX * SPLIT, TILE)
+
+        def block(start):
+            return lambda r: field[seg][8 * r : 8 * r + 8, lanes(start, 128)]
 
         for k in range(6):
-            if (half, k) in BY_LANES:
-                links = nbr[k : k + 1, cells]
-                sets = jnp.where(links >= EXT, NEAR_BLOCKS - 1, (links >> 7) - 4 * a)
-                found = turn_lanes(block, links & 127, sets)
-            else:
-                found = pick(table, ohn[k, c], sidn[k : k + 1, cells], NEAR)
+            links = nbr[k : k + 1, cells]
+            sets = jnp.broadcast_to(sidn[k : k + 1, cells], (8, TILE))
+            found = pick(table, ohn[k, c], sets, BY_MATRIX)
+            place = links & 127
+            for s in range(2 * BY_MATRIX, NEAR_BLOCKS - 1):
+                start = a * RIM + s * 128
+                found = from_block(block(start), place, jnp.broadcast_to(links >> 7, (8, TILE)) == 4 * a + s, found)
+            found = from_block(block(EXT + a * AXIAL), place, sets == NEAR - 1, found)
             face = jnp.broadcast_to(area[k : k + 1, cells], (8, TILE))
             jump = [(found[r] - own[r]) * face for r in range(ROWS // 8)]
             for v in range(NV):
@@ -404,11 +393,6 @@
 
         for a in group:
             radial_copy(seg, a).wait_recv()
-            high, low = halves(field[seg][:, lanes(EXT + a * AXIAL, AXIAL)])
-            across = (12 + a // 2) * SPLIT
-            column = lanes(a % 2 * AXIAL, AXIAL)
-            near[side][pl.ds(pl.multiple_of(across, 16), ROWS), column] = high
-            near[side][pl.ds(pl.multiple_of(across + ROWS, 16), ROWS), column] = low
 
         for a in group:
             for half in range(2):
@@ -464,11 +448,11 @@
             pltpu.VMEM((GROUP, ROWS, 128), F32),
             pltpu.VMEM((GROUP, ROWS, 128), F32),
             pltpu.VMEM((GROUP, ROWS, 128), F32),
-            pltpu.VMEM((SOURCES * SPLIT, TILE), BF16),
+            pltpu.VMEM((SPLIT // 16, SOURCES * 16, TILE), BF16),
             pltpu.VMEM((2, TILES, TILE, TILE), BF16),
             pltpu.VMEM((6, TILES, TILE, TILE), BF16),
-            pltpu.VMEM((14 * SPLIT, TILE), BF16),
-            pltpu.VMEM((14 * SPLIT, TILE), BF16),
+            pltpu.VMEM((SPLIT // 16, 12 * 16, TILE), BF16),
+            pltpu.VMEM((SPLIT // 16, 12 * 16, TILE), BF16),
             pltpu.VMEM((6, CELLS), jnp.int32),
             pltpu.VMEM((2, CELLS), jnp.int32),
             pltpu.VMEM((ROWS, CELLS + 3 * RIM), F32),

time: 53.4 us -> 51.9 us (0.972)
  the two profiles are of different devices: /device:TPU:2 before, /device:TPU:4 now
where the time goes in v5:
time: 51.9 us; the launch traced here: 51.8 us
  Pallas kernels  50.3 us (97%)
  local copies, waits for them, and re-layouts  0.82 us (2%)
  between operations  0.66 us (1%)
    pallas_call x1, Pallas kernels, per_device(): pl.pallas_call(kernel, out_shape=jax.ShapeDtypeStruct((NI, NV, CELLS), F3...  50.3 us

profile of v5, /device:TPU:4, one launch (start us, length us, event | category | flops | bytes accessed | tf_op | source)
XLA Modules:
  0.0 51.8 jit_solution(9328446221578141182)
XLA Ops:
  0.7 50.3 %grid_sequence.1 = f32[9,5,2048]{2,1,0:T(8,128)S(1)} custom-call(f32[9,5,256]{2,1,0:T(8,128)} %bitcast.6, s32[1,2048]{1,0:T(1,128)} %send_in.1, s32[2,2048]{1,0:T(2,128)} %fsrc_in.1, f32[1,2048]{1,0:T(1,128)} %bitcast.8, s32[6,2048]{1,0:T(8,128)} %nbr_in.1, f32[6,2048]{1,0:T(8,128)} %area_in.1, f32[1,2048]{1,0:T(1,128)} %bitcast.9, f32[5,6,5]{2,1,0:T(8,128)} %bitcast.7, ...), custom_call_target="tpu_custom_call" | custom-call | tf_op jit(solution)/shard_map/grid_sequence/pallas_call | solution.py:430
  51.0 0.8 %copy.13 = f32[5,9,2048]{2,0,1:T(8,128)} copy(f32[5,9,2048]{2,0,1:T(8,128)S(1)} %bitcast.5) | data formatting | bytes 737280

commit v6 on v5

--- a/solution.py
+++ b/solution.py
@@ -22,7 +22,6 @@
 TILES = CELLS // TILE
 NEAR = 7
 NEAR_BLOCKS = 13
-TOGETHER = 1
 BY_MATRIX = 5
 GROUP = 16
 CHUNK = 24
@@ -90,7 +89,7 @@
 
 def kernel(
     coarse_in, send_in, fsrc_in, weight_in, nbr_in, area_in, dt_in, mix_in, freq_in, dmat_in, out,
-    coarse, send, fsrc, weight, nbr, area, dt, mix, freq, dmat, isem, outg, recv1, send2, recv2, rtab, ohs, ohn, near0, near1, sidn, sids, field0, field1, field2, field3, mixcol,
+    coarse, send, fsrc, weight, nbr, area, dt, mix, freq, dmat, isem, outg, recv1, send2, recv2, rtab, ohs, ohn, near0, near1, sidn, sids, field0, field1, field2, mixcol,
     ssem1, rsem1, ssem2, rsem2, hssem, hrsem,
 ):
     inputs = [
@@ -105,7 +104,7 @@
     for copy in inputs:
         copy.start()
 
-    field = [field0, field1, field2, field3]
+    field = [field0, field1, field2]
     near = [near0, near1]
     t = lax.axis_index("theta")
     i = lax.axis_index("inst")
@@ -129,6 +128,8 @@
     def lanes(start, size):
         return pl.ds(pl.multiple_of(start, 128), size)
 
+    for arriving in (recv1, recv2):
+        arriving[:, ROWS - 8 :, :] = jnp.zeros((GROUP, 8, 128), F32)
     barrier = pltpu.get_barrier_semaphore()
 
     def greet(s, carry):
@@ -150,7 +151,7 @@
 
     lane = lax.broadcasted_iota(jnp.int32, (8, 128), 1)
 
-    def gather_out(c, carry):
+    for c in range(TILES):
         even = send[:, lanes(c * TILE, 128)]
         odd = send[:, lanes(c * TILE + 128, 128)]
         keep = (lane[:1] & 16) == 0
@@ -161,14 +162,11 @@
         found = found[:ROWS] + found[ROWS:]
         outg[2 * c] = found[:, :128]
         outg[2 * c + 1] = found[:, 128:]
-        return carry
-
-    lax.fori_loop(0, TILES, gather_out, 0)
 
     pl.semaphore_wait(barrier, 2 * (GROUP - 1) + 2)
 
     def phase1(c, s):
-        part = pl.ds(c * CHUNK, CHUNK)
+        part = pl.ds(c * CHUNK, min(CHUNK, NV * NI - c * CHUNK))
         return pltpu.make_async_remote_copy(
             src_ref=outg.at[(g + s) % GROUP, part],
             dst_ref=recv1.at[g, part],
@@ -179,7 +177,7 @@
         )
 
     def phase2(c, s):
-        part = pl.ds(c * CHUNK, CHUNK)
+        part = pl.ds(c * CHUNK, min(CHUNK, NV * NI - c * CHUNK))
         return pltpu.make_async_remote_copy(
             src_ref=send2.at[(h + s) % GROUP, part],
             dst_ref=recv2.at[h, part],
@@ -288,14 +286,14 @@
             device_id_type=MESH,
         )
 
-    def send_layer(seg, j, a):
+    def send_layer(seg, a):
         radial_copy(seg, a).start()
 
-        @pl.when(j == 2)
+        @pl.when(a == 0)
         def _():
             behind_copy(seg).start()
 
-        @pl.when(j == 3)
+        @pl.when(a == LAYERS - 1)
         def _():
             ahead_copy(seg).start()
 
@@ -304,14 +302,15 @@
             for r in range(ROWS // 16):
                 near[side][2 * r + half, pl.ds(pl.multiple_of(at * 16, 16), 16), :] = part[16 * r : 16 * r + 16]
 
-    def layer_of(j):
-        return jnp.where(j < 2, j + 1, (j - 2) * 3)
+    def layer_of(seg, j):
+        outer = (j - 2) * 3 if seg % 2 == 0 else (3 - j) * 3
+        return jnp.where(j < 2, j + 1, outer)
 
     for copy in inputs[5:]:
         copy.wait()
 
     def start_layer(j, carry):
-        a = layer_of(j)
+        a = layer_of(1, j)
         for half in range(2):
             c = 2 * a + half
             cells = lanes(c * TILE, TILE)
@@ -322,7 +321,7 @@
             for r in range(ROWS // 8):
                 field[0][8 * r : 8 * r + 8, lanes(RIM + c * TILE, TILE)] = begin[r]
             put(0, 2 + c, begin)
-        send_layer(0, j, a)
+        send_layer(0, a)
         return carry
 
     lax.fori_loop(0, LAYERS, start_layer, 0)
@@ -365,54 +364,46 @@
             rate[NV] = rate[NV] - last
         step = jnp.broadcast_to(coef * dt[:, cells], (8, TILE))
         after = [field[0][8 * r : 8 * r + 8, here] - step * rate[r] for r in range(ROWS // 8)]
-        for r in range(ROWS // 8):
-            field[seg + 1][8 * r : 8 * r + 8, here] = after[r]
         if seg < 2:
+            for r in range(ROWS // 8):
+                field[seg + 1][8 * r : 8 * r + 8, here] = after[r]
             put(1 - side, 2 + c, after)
-
-    def rate_layers(seg, step_at):
+        else:
+            for v in range(NV):
+                out[0:8, v, cells] = after[v]
+            out[8, :, cells] = after[NV][:NV]
+
+    def rate_layer(seg, j):
         side = seg % 2
-        coef = SEGMENT_COEFS[seg]
-        group = [layer_of(step_at * TOGETHER + n) for n in range(TOGETHER)]
+        a = layer_of(seg, j)
 
         def arrived(start, at_set):
             for half in range(2):
                 put(side, at_set + half, [field[seg][:, start + half * TILE : start + (half + 1) * TILE]])
 
-        for n in range(TOGETHER):
-
-            @pl.when(step_at * TOGETHER + n == 2)
-            def _():
-                ahead_copy(seg).wait_recv()
-                arrived(0, 0)
-
-            @pl.when(step_at * TOGETHER + n == 3)
-            def _():
-                behind_copy(seg).wait_recv()
-                arrived(RIM + CELLS, 10)
-
-        for a in group:
-            radial_copy(seg, a).wait_recv()
-
-        for a in group:
-            for half in range(2):
-                rate_tile(seg, side, coef, a, half)
-
+        @pl.when(a == 0)
+        def _():
+            ahead_copy(seg).wait_recv()
+            arrived(0, 0)
+
+        @pl.when(a == LAYERS - 1)
+        def _():
+            behind_copy(seg).wait_recv()
+            arrived(RIM + CELLS, 10)
+
+        radial_copy(seg, a).wait_recv()
+        for half in range(2):
+            rate_tile(seg, side, SEGMENT_COEFS[seg], a, half)
         if seg < 2:
-            for n in range(TOGETHER):
-                send_layer(seg + 1, step_at * TOGETHER + n, group[n])
+            send_layer(seg + 1, a)
 
     for seg in range(3):
 
-        def rate_step(step_at, carry):
-            rate_layers(seg, step_at)
+        def rate_step(j, carry):
+            rate_layer(seg, j)
             return carry
 
-        lax.fori_loop(0, LAYERS // TOGETHER, rate_step, 0)
-
-    for v in range(NV):
-        out[0:8, v, :] = field[3][8 * v : 8 * v + 8, RIM : RIM + CELLS]
-    out[8] = field[3][8 * NV : 9 * NV, RIM : RIM + CELLS]
+        lax.fori_loop(0, LAYERS, rate_step, 0)
 
     for c in range(CHUNKS):
         each(lambda s: phase1(c, s).wait_send())
@@ -458,7 +449,6 @@
             pltpu.VMEM((ROWS, CELLS + 3 * RIM), F32),
             pltpu.VMEM((ROWS, CELLS + 3 * RIM), F32),
             pltpu.VMEM((ROWS, CELLS + 3 * RIM), F32),
-            pltpu.VMEM((ROWS, CELLS + 3 * RIM), F32),
             pltpu.VMEM((6, NV, 8, 128), F32),
             pltpu.SemaphoreType.DMA((CHUNKS, GROUP)),
             pltpu.SemaphoreType.DMA((CHUNKS, GROUP)),

time: 51.9 us -> 50.7 us (0.977)
  the two profiles are of different devices: /device:TPU:4 before, /device:TPU:2 now
where the time goes in v6:
time: 50.7 us; the launch traced here: 50.2 us
  Pallas kernels  48.7 us (96%)
  local copies, waits for them, and re-layouts  0.82 us (2%)
  between operations  0.66 us (1%)
    pallas_call x1, Pallas kernels, per_device(): pl.pallas_call(kernel, out_shape=jax.ShapeDtypeStruct((NI, NV, CELLS), F3...  48.7 us

profile of v6, /device:TPU:2, one launch (start us, length us, event | category | flops | bytes accessed | tf_op | source)
XLA Modules:
  0.0 50.2 jit_solution(15668062554836247429)
XLA Ops:
  0.7 48.7 %grid_sequence.1 = f32[9,5,2048]{2,1,0:T(8,128)S(1)} custom-call(f32[9,5,256]{2,1,0:T(8,128)} %bitcast.6, s32[1,2048]{1,0:T(1,128)} %send_in.1, s32[2,2048]{1,0:T(2,128)} %fsrc_in.1, f32[1,2048]{1,0:T(1,128)} %bitcast.8, s32[6,2048]{1,0:T(8,128)} %nbr_in.1, f32[6,2048]{1,0:T(8,128)} %area_in.1, f32[1,2048]{1,0:T(1,128)} %bitcast.9, f32[5,6,5]{2,1,0:T(8,128)} %bitcast.7, ...), custom_call_target="tpu_custom_call" | custom-call | tf_op jit(solution)/shard_map/grid_sequence/pallas_call | solution.py:421
  49.4 0.8 %copy.13 = f32[5,9,2048]{2,0,1:T(8,128)} copy(f32[5,9,2048]{2,0,1:T(8,128)S(1)} %bitcast.5) | data formatting | bytes 737280

commit v7 on v6

--- a/solution.py
+++ b/solution.py
@@ -26,6 +26,7 @@
 GROUP = 16
 CHUNK = 24
 CHUNKS = ROWS // CHUNK
+FIRST = (8, 7, 9, 6, 10, 5, 11, 4, 12, 3, 13, 2, 14, 1, 15)
 SOURCES = 8
 
 SEGMENT_COEFS = (0.6, 0.6, 1.0)
@@ -192,7 +193,8 @@
             action(s)
 
     for c in range(CHUNKS):
-        each(lambda s: phase1(c, s).start())
+        for s in FIRST:
+            phase1(c, s).start()
     recv1[g] = outg[g]
 
     for copy in inputs[2:5]:

time: 50.7 us -> 50.2 us (level)
    pallas_call x1, Pallas kernels: 48.7 us -> 48.2 us  [per_device(): pl.pallas_call(kernel, out_shape=jax.ShapeDtypeStruct((NI, NV, CELLS), F3...]
where the time goes in v7:
time: 50.2 us; the launch traced here: 49.7 us
  Pallas kernels  48.2 us (96%)
  local copies, waits for them, and re-layouts  0.82 us (2%)
  between operations  0.66 us (1%)
    pallas_call x1, Pallas kernels, per_device(): pl.pallas_call(kernel, out_shape=jax.ShapeDtypeStruct((NI, NV, CELLS), F3...  48.2 us

profile of v7, /device:TPU:2, one launch (start us, length us, event | category | flops | bytes accessed | tf_op | source)
XLA Modules:
  0.0 49.7 jit_solution(18116392402474690191)
XLA Ops:
  0.7 48.2 %grid_sequence.1 = f32[9,5,2048]{2,1,0:T(8,128)S(1)} custom-call(f32[9,5,256]{2,1,0:T(8,128)} %bitcast.6, s32[1,2048]{1,0:T(1,128)} %send_in.1, s32[2,2048]{1,0:T(2,128)} %fsrc_in.1, f32[1,2048]{1,0:T(1,128)} %bitcast.8, s32[6,2048]{1,0:T(8,128)} %nbr_in.1, f32[6,2048]{1,0:T(8,128)} %area_in.1, f32[1,2048]{1,0:T(1,128)} %bitcast.9, f32[5,6,5]{2,1,0:T(8,128)} %bitcast.7, ...), custom_call_target="tpu_custom_call" | custom-call | tf_op jit(solution)/shard_map/grid_sequence/pallas_call | solution.py:423
  48.9 0.8 %copy.13 = f32[5,9,2048]{2,0,1:T(8,128)} copy(f32[5,9,2048]{2,0,1:T(8,128)S(1)} %bitcast.5) | data formatting | bytes 737280

commit v8 on v7

--- a/solution.py
+++ b/solution.py
@@ -245,7 +245,8 @@
                         x[a], x[b] = low, high
             for j in range(GROUP):
                 send2[j, part, :] = x[j]
-        each(lambda s: phase2(c, s).start())
+        for s in FIRST:
+            phase2(c, s).start()
     recv2[h] = send2[h]
     for c in range(CHUNKS):
         each(lambda s: phase2(c, s).wait_recv())

time: 50.2 us -> 50.2 us (level)
  no operation moved by 1% of the time
where the time goes in v8:
time: 50.2 us; the launch traced here: 49.2 us
  Pallas kernels  47.8 us (95%)
  local copies, waits for them, and re-layouts  0.82 us (2%)
  between operations  0.66 us (1%)
    pallas_call x1, Pallas kernels, per_device(): pl.pallas_call(kernel, out_shape=jax.ShapeDtypeStruct((NI, NV, CELLS), F3...  47.8 us

profile of v8, /device:TPU:2, one launch (start us, length us, event | category | flops | bytes accessed | tf_op | source)
XLA Modules:
  0.0 49.2 jit_solution(9946040961915339714)
XLA Ops:
  0.7 47.8 %grid_sequence.1 = f32[9,5,2048]{2,1,0:T(8,128)S(1)} custom-call(f32[9,5,256]{2,1,0:T(8,128)} %bitcast.6, s32[1,2048]{1,0:T(1,128)} %send_in.1, s32[2,2048]{1,0:T(2,128)} %fsrc_in.1, f32[1,2048]{1,0:T(1,128)} %bitcast.8, s32[6,2048]{1,0:T(8,128)} %nbr_in.1, f32[6,2048]{1,0:T(8,128)} %area_in.1, f32[1,2048]{1,0:T(1,128)} %bitcast.9, f32[5,6,5]{2,1,0:T(8,128)} %bitcast.7, ...), custom_call_target="tpu_custom_call" | custom-call | tf_op jit(solution)/shard_map/grid_sequence/pallas_call | solution.py:424
  48.4 0.8 %copy.13 = f32[5,9,2048]{2,0,1:T(8,128)} copy(f32[5,9,2048]{2,0,1:T(8,128)S(1)} %bitcast.5) | data formatting | bytes 737280
